TPU v7x, 256 devices: a whole 4x4x8 slice. The times are simulated.
256 devices in a mesh: dom: 64 (over z, x, core), grp: 4 (over y).
Axes of the slice: x: 4, y: 4, z: 8, core: 2. Of those that a mesh axis runs over, the one named last changes fastest.
Arguments:
- initial: bfloat16 [4, 32768, 512], P('grp', 'dom'), may hold values from -6 to 6
- history: bfloat16 [4, 32768, 512], P('grp', 'dom'), may hold values from 0 to 2
- tile_values: bfloat16 [4, 256, 8, 128, 128], P('grp', 'dom'), may hold values from -0.1875 to 0.1875
- tile_cols: int32 [4, 256, 8], P('grp', 'dom'), may hold values from 0 to 67
- send_blocks: int32 [4, 64, 64], P('grp', 'dom'), may hold values from 0 to 3
- weight_one: bfloat16 [512, 512], replicated, may hold values from -0.25 to 0.25
- weight_two: bfloat16 [512, 512], replicated, may hold values from -0.25 to 0.25
- cotangent: bfloat16 [4, 32768, 512], P('grp', 'dom'), may hold values from -6 to 6
Outputs:
- embeddings: bfloat16 [4, 32768, 512], P('grp', 'dom')
- grad_one: float32 [512, 512], replicated
- grad_two: float32 [512, 512], replicated
All inputs are finite; a program needn't handle non-finite values.
Results may differ from a plain program's by a relative error of at most 0.0071.
Values may be sent and summed in bfloat16 or wider, within the bound.
A program may use at most 128 MiB of HBM per device.

v0:
```python
import jax
import jax.numpy as jnp
from jax import lax
from jax.sharding import PartitionSpec as P

RESTART = 0.1
BETA_ONE = 0.405465
BETA_TWO = 0.223144


def silu_slope(value):
    sig = jax.nn.sigmoid(value)
    return sig * (1.0 + value * (1.0 - sig))


def propagate(tile_part, col_part, own_blocks, received):
    buffer = jnp.concatenate([own_blocks, received], axis=0)
    picked = buffer[col_part]
    return jnp.einsum("rkij,rkjd->rid", tile_part, picked, preferred_element_type=jnp.float32)


def local_transpose(tile_part, col_part, back_blocks):
    count = tile_part.shape[0]
    slots = tile_part.shape[1]
    size = tile_part.shape[2]
    width = back_blocks.shape[2]
    flat_cols = col_part.reshape(count * slots)
    is_local = (flat_cols < count).astype(jnp.int32)
    order = jnp.argsort(1 - is_local, stable=True)
    local_count = jnp.sum(is_local)

    def add_tile(turn, total):
        where = order[turn]
        row_block = where // slots
        slot = where % slots
        column = flat_cols[where]
        tile = lax.dynamic_index_in_dim(
            lax.dynamic_index_in_dim(tile_part, row_block, 0, keepdims=False),
            slot,
            0,
            keepdims=False,
        )
        rows = lax.dynamic_index_in_dim(back_blocks, row_block, 0, keepdims=False)
        term = lax.dot_general(
            tile, rows, (((0,), (0,)), ((), ())), preferred_element_type=jnp.float32
        )
        current = lax.dynamic_index_in_dim(total, column, 0, keepdims=True)
        return lax.dynamic_update_index_in_dim(total, current + term[None], column, 0)

    start = jnp.zeros((count, size, width), jnp.float32)
    return lax.fori_loop(0, local_count, add_tile, start)


def local(initial, history, tile_values, tile_cols, send_blocks, weight_one, weight_two, cotangent):
    tile_part = tile_values[0]
    col_part = tile_cols[0]
    count = tile_part.shape[0]
    size = tile_part.shape[2]
    width = initial.shape[2]
    own_blocks = initial[0].reshape(count, size, width)
    past_blocks = history[0].reshape(count, size, width)
    chosen = send_blocks[0, 0]
    outgoing_in = own_blocks[chosen]
    outgoing_past = past_blocks[chosen]
    received_in, received_past = (
        lax.all_to_all(outgoing_in, "dom", split_axis=0, concat_axis=0, tiled=True),
        lax.all_to_all(outgoing_past, "dom", split_axis=0, concat_axis=0, tiled=True),
    )
    own_float = own_blocks.astype(jnp.float32)
    mixed_one = (
        (1.0 - RESTART) * propagate(tile_part, col_part, own_blocks, received_in)
        + RESTART * own_float
    ).astype(jnp.bfloat16)
    flat_one = mixed_one.reshape(count * size, width)
    pre_one = (1.0 - BETA_ONE) * flat_one.astype(jnp.float32) + BETA_ONE * jnp.dot(
        flat_one, weight_one, preferred_element_type=jnp.float32
    )
    hidden_one = jax.nn.silu(pre_one).astype(jnp.bfloat16)
    mixed_two = (
        (1.0 - RESTART)
        * propagate(tile_part, col_part, hidden_one.reshape(count, size, width), received_past)
        + RESTART * own_float
    ).astype(jnp.bfloat16)
    flat_two = mixed_two.reshape(count * size, width)
    pre_two = (1.0 - BETA_TWO) * flat_two.astype(jnp.float32) + BETA_TWO * jnp.dot(
        flat_two, weight_two, preferred_element_type=jnp.float32
    )
    output = jax.nn.silu(pre_two).astype(jnp.bfloat16)
    cot_flat = cotangent[0]
    back_two = (cot_flat.astype(jnp.float32) * silu_slope(pre_two)).astype(jnp.bfloat16)
    grad_two = BETA_TWO * jnp.einsum(
        "nd,ne->de", flat_two, back_two, preferred_element_type=jnp.float32
    )
    back_mixed = (
        (1.0 - BETA_TWO) * back_two.astype(jnp.float32)
        + BETA_TWO * jnp.dot(back_two, weight_two.T, preferred_element_type=jnp.float32)
    ).astype(jnp.bfloat16)
    back_hidden = (1.0 - RESTART) * local_transpose(
        tile_part, col_part, back_mixed.reshape(count, size, width)
    )
    back_one = (back_hidden.reshape(count * size, width) * silu_slope(pre_one)).astype(jnp.bfloat16)
    grad_one = BETA_ONE * jnp.einsum(
        "nd,ne->de", flat_one, back_one, preferred_element_type=jnp.float32
    )
    grad_one, grad_two = lax.psum((grad_one, grad_two), ("dom", "grp"))
    return (output.reshape(1, count * size, width), grad_one, grad_two)


def solution(mesh):
    return jax.shard_map(
        local,
        mesh=mesh,
        in_specs=(
            P("grp", "dom", None),
            P("grp", "dom", None),
            P("grp", "dom", None, None, None),
            P("grp", "dom", None),
            P("grp", "dom", None),
            P(),
            P(),
            P("grp", "dom", None),
        ),
        out_specs=(P("grp", "dom", None), P(), P()),
        check_vma=False,
    )
```

profile of v0, /device:TPU:1, one launch (start us, length us, event | category | flops | bytes accessed | tf_op | source)
XLA Modules:
  0.0 754.0 jit_solution(1007423749495553562)
XLA Ops:
  7.2 0.7 fusion.23
  7.9 6.5 gather_fusion
  14.4 13.1 %all-to-all-start = ((bf16[64,128,512]{2,1,0:T(8,128)(2,1)}), bf16[64,128,512]{2,1,0:T(8,128)(2,1)}, u32[]{:S(2)}, u32[]{:S(2)}) async-start(bf16[64,128,512]{2,1,0:T(8,128)(2,1)} %gather_fusion), calls=%async_computation | async-start | bytes 16777216 | tf_op jit(solution)/shard_map/all_to_all | solution.py:66
  27.6 5.5 gather_fusion.2
  33.1 176.9 %all-to-all-done = bf16[64,128,512]{2,1,0:T(8,128)(2,1)} async-done(((bf16[64,128,512]{2,1,0:T(8,128)(2,1)}), bf16[64,128,512]{2,1,0:T(8,128)(2,1)}, u32[]{:S(2)}, u32[]{:S(2)}) %all-to-all-start) | async-done | bytes 8388640 | tf_op jit(solution)/shard_map/all_to_all | solution.py:66
  209.9 10.2 %all-to-all-start.1 = ((bf16[64,128,512]{2,1,0:T(8,128)(2,1)}), bf16[64,128,512]{2,1,0:T(8,128)(2,1)}, u32[]{:S(2)}, u32[]{:S(2)}) async-start(bf16[64,128,512]{2,1,0:T(8,128)(2,1)} %gather_fusion.2), calls=%async_computation.1 | async-start | bytes 16777216 | tf_op jit(solution)/shard_map/all_to_all | solution.py:67
  220.2 0.1 reshape_squeeze.11
  220.3 0.1 reshape.101
  220.4 1.6 sort.17
  222.0 0.7 convert_reduce_fusion
  222.8 7.6 %pad_maximum_fusion = bf16[68,128,512]{2,1,0:T(8,128)(2,1)} fusion(bf16[64,128,512]{2,1,0:T(8,128)(2,1)} %all-to-all-done, bf16[4,128,512]{2,1,0:T(8,128)(2,1)S(1)} %bitcast.102), kind=kLoop, calls=%fused_computation.12 | loop fusion | flops 4456448 | bytes 17825792 | tf_op jit(solution)/shard_map/concatenate | solution.py:17
  230.3 6.4 gather_fusion.1
  236.8 2.9 fusion.17
  239.7 2.6 multiply_convert_fusion.1
  242.3 160.2 %all-to-all-done.1 = bf16[64,128,512]{2,1,0:T(8,128)(2,1)} async-done(((bf16[64,128,512]{2,1,0:T(8,128)(2,1)}), bf16[64,128,512]{2,1,0:T(8,128)(2,1)}, u32[]{:S(2)}, u32[]{:S(2)}) %all-to-all-start.1) | async-done | bytes 8388640 | tf_op jit(solution)/shard_map/all_to_all | solution.py:67
  402.6 7.6 %pad_maximum_fusion.1 = bf16[68,128,512]{2,1,0:T(8,128)(2,1)} fusion(bf16[64,128,512]{2,1,0:T(8,128)(2,1)} %all-to-all-done.1, bf16[4,128,512]{2,1,0:T(8,128)(2,1)S(1)} %bitcast.113), kind=kLoop, calls=%fused_computation.13 | loop fusion | flops 4456448 | bytes 17825792 | tf_op jit(solution)/shard_map/concatenate | solution.py:17
  410.2 6.4 gather_fusion.3
  416.6 3.0 fusion.18
  419.6 2.7 fusion.19
  422.2 1.3 fusion.16
  423.5 1.4 convolution_multiply_fusion
  424.9 0.1 broadcast_in_dim.14
  425.1 10.0 %while.13 = (s32[]{:T(128)}, f32[4,128,512]{2,1,0:T(8,128)S(1)}, s32[]{:T(128)}, s32[32]{0:T(128)S(1)}, s32[32]{0:T(128)S(1)}, /*index=5*/bf16[4,8,128,128]{3,2,...) while((s32[]{:T(128)}, f32[4,128,512]{2,1,0:T(8,128)S(1)}, ...), condition=%wide.region_3.4_spmd, body=%wide.region_2.3_spmd.sunk | while | flops 16842788 | bytes 688689 | solution.py:51
  425.8 0.7 dynamic_slice.53
  430.6 0.7 dynamic_slice.54
  433.3 1.1 fusion.43
  435.1 0.1 broadcast_multiply_fusion
  435.2 1.7 fusion.20
  436.9 1.4 convolution_multiply_fusion.1
  438.4 304.3 %all-reduce.3.cloned.1.call-done = (f32[512,512]{1,0:T(8,128)}, f32[512,512]{1,0:T(8,128)}) async-done(((f32[512,512]{1,0:T(8,128)}, f32[512,512]{1,0:T(8,128)}), (f32[512,512]{1,0:T(8,128)}, f32[512,512]{1,0:T(8,128)})) %all-reduce.3.cloned.1.call-update) | async-done | bytes 2097168 | tf_op jit(solution)/shard_map/psum | solution.py:105
  742.7 2.3 copy.22
  744.9 2.3 copy.23
  (21 shorter events, 0.1 us)
Async XLA Ops:
  7.2 20.4 %copy-start = (bf16[1,512,512]{2,1,0:T(8,128)(2,1)S(1)}, bf16[1,512,512]{2,1,0:T(8,128)(2,1)}, u32[]{:S(2)}) copy-start(bf16[1,512,512]{2,1,0:T(8,128)(2,1)} %param.11) | copy-start | bytes 1572868
  14.4 195.5 %all-to-all-start = ((bf16[64,128,512]{2,1,0:T(8,128)(2,1)}), bf16[64,128,512]{2,1,0:T(8,128)(2,1)}, u32[]{:S(2)}, u32[]{:S(2)}) async-start(bf16[64,128,512]{2,1,0:T(8,128)(2,1)} %gather_fusion), calls=%async_computation | async-start | bytes 16777216 | tf_op jit(solution)/shard_map/all_to_all | solution.py:66
  33.1 187.2 %copy-start.4 = (s32[1,4,8]{2,1,0:T(4,128)S(1)}, s32[1,4,8]{2,1,0:T(4,128)}, u32[]{:S(2)}) copy-start(s32[1,4,8]{2,1,0:T(4,128)} %param.13) | copy-start | bytes 388
  33.1 189.7 %copy-start.2 = (bf16[1,512,512]{2,1,0:T(8,128)(2,1)S(1)}, bf16[1,512,512]{2,1,0:T(8,128)(2,1)}, u32[]{:S(2)}) copy-start(bf16[1,512,512]{2,1,0:T(8,128)(2,1)} %param.10) | copy-start | bytes 1572868
  209.9 192.6 %all-to-all-start.1 = ((bf16[64,128,512]{2,1,0:T(8,128)(2,1)}), bf16[64,128,512]{2,1,0:T(8,128)(2,1)}, u32[]{:S(2)}, u32[]{:S(2)}) async-start(bf16[64,128,512]{2,1,0:T(8,128)(2,1)} %gather_fusion.2), calls=%async_computation.1 | async-start | bytes 16777216 | tf_op jit(solution)/shard_map/all_to_all | solution.py:67
  220.2 522.5 %all-reduce.3.cloned.1.call-start = ((), (), s32[]{:S(2)}) async-start(), calls=%async_computation.2 | async-start | bytes 4194304 | tf_op jit(solution)/shard_map/psum | solution.py:105
  230.3 6.4 copy-start.3
  410.2 9.4 %copy-start.5 = (bf16[1,512,512]{2,1,0:T(8,128)(2,1)S(1)}, bf16[1,512,512]{2,1,0:T(8,128)(2,1)}, u32[]{:S(2)}) copy-start(bf16[1,512,512]{2,1,0:T(8,128)(2,1)} %param.17) | copy-start | bytes 1572868
  416.6 5.7 copy-start.6
  425.1 322.1 %copy-start.1 = (bf16[1,512,512]{2,1,0:T(8,128)(2,1)S(1)}, bf16[1,512,512]{2,1,0:T(8,128)(2,1)}, u32[]{:S(2)}) copy-start(bf16[1,512,512]{2,1,0:T(8,128)(2,1)} %param.11) | copy-start | bytes 1572868
Sparse Core Ops, SparseCore 0:
  438.5 304.1 all-reduce.2
where the time goes:
time: 756 us; the launch traced here: 754 us
  waiting for transfers between devices  641 us (85%)
  local copies, waits for them, and re-layouts  31 us (4%)
  starting transfers between devices  23.4 us (3%)
  other arithmetic  20 us (3%)
  matrix products  16.5 us (2%)
  between operations  14.1 us (2%)
  loops' own time  7.61 us (1%)
    psum x1, waiting for transfers between devices, local(): grad_one, grad_two = lax.psum((grad_one, grad_two), ('dom', 'grp'))  304 us
    all_to_all x1, waiting for transfers between devices, local(): lax.all_to_all(outgoing_in, 'dom', split_axis=0, concat_axis=0, tiled=True)  177 us
    all_to_all x1, waiting for transfers between devices, local(): lax.all_to_all(outgoing_past, 'dom', split_axis=0, concat_axis=0, tiled=T...  160 us
    concatenate x2, other arithmetic, propagate(): buffer = jnp.concatenate([own_blocks, received], axis=0)  15.2 us
  transfers between devices with their start and end apart: 3, of which 3 were waited for; matrix products, arithmetic and copies ran while one was open for 4% of the time, Pallas kernels for 0%

commit v1 on v0

v1 whole, which is shorter than its diff:
```python
import functools

import jax
import jax.numpy as jnp
from jax import lax
from jax.experimental import pallas as pl
from jax.experimental.pallas import tpu as pltpu
from jax.sharding import PartitionSpec as P

RESTART = 0.1
BETA_ONE = 0.405465
BETA_TWO = 0.223144

NZ = 8
NX = 4
NY = 4
STAGES = 4
MESH = pl.DeviceIdType.MESH


def dom_index(z, x, core):
    return (z * NX + x) * 2 + core


def exchange_kernel(
    initial_ref, history_ref, tiles_ref, meta_ref, out_ref,
    feat0, feat1, feat2, feat3, tiles_all, part_out, part_in, metas, metas_smem, table,
    z_recv, sib_recv, z_send, own_sem, t_recv, t_far, t_sib, t_send, t_own, p_recv, p_send,
    m_recv, m_send, m_copy,
):
    feats = (feat0, feat1, feat2, feat3)
    blocks, size, _ = initial_ref.shape
    slots = tiles_ref.shape[1]
    wide = feat0.shape[2]
    dom = lax.axis_index("dom")
    core = lax.rem(dom, 2)
    my_x = lax.rem(dom // 2, NX)
    my_z = dom // (2 * NX)
    other = 1 - core

    def at(dz, dx, flip):
        z = lax.rem(my_z + dz, NZ)
        x = lax.rem(my_x + dx, NX)
        return {"dom": dom_index(z, x, other if flip else core)}

    row = [(0, dx, f) for dx in range(NX) for f in range(2) if (dx, f) != (0, 0)]
    column = [(dz, 0, f) for dz in range(1, NZ) for f in range(2)]
    barrier = pltpu.get_barrier_semaphore()
    for peer in row + column:
        pl.semaphore_signal(barrier, inc=1, device_id=at(*peer), device_id_type=MESH)
    pl.semaphore_wait(barrier, len(row) + len(column))

    def remote(src, dst, send_sem, recv_sem, peer):
        return pltpu.make_async_remote_copy(
            src_ref=src, dst_ref=dst, send_sem=send_sem, recv_sem=recv_sem,
            device_id=at(*peer), device_id_type=MESH,
        )

    def feat_slot(stage, dz, flip):
        return feats[stage].at[pl.ds((dz * 2 + flip) * blocks, blocks)]

    def own_columns(stage, flip):
        ref = (initial_ref, history_ref)[stage // 2]
        half = other if flip else core
        start = pl.multiple_of((half * 2 + stage % 2) * wide, wide)
        return ref.at[:, :, pl.ds(start, wide)]

    def start_stage(stage):
        for flip in range(2):
            for direction, dz in ((0, 1), (1, NZ - 1)):
                remote(
                    own_columns(stage, flip), feat_slot(stage, NZ - dz, flip),
                    z_send.at[stage], z_recv.at[stage, direction, flip], (dz, 0, flip),
                ).start()
        remote(
            own_columns(stage, 1), feat_slot(stage, 0, 1),
            z_send.at[stage], sib_recv.at[stage], (0, 0, 1),
        ).start()
        pltpu.make_async_copy(own_columns(stage, 0), feat_slot(stage, 0, 0), own_sem.at[stage]).start()

    def land(ref, sem):
        pltpu.make_async_copy(ref, ref, sem).wait()

    def ring_tick(stage, m):
        for direction, dz in ((0, 1), (1, NZ - 1)):
            hop = m // 2 + 1
            flip = m % 2 if hop < NZ // 2 else direction
            origin = (NZ - hop if direction == 0 else hop) % NZ
            slot = feat_slot(stage, origin, flip)
            land(slot, z_recv.at[stage, direction, m])
            if hop < NZ // 2 - 1 or (hop == NZ // 2 - 1 and flip == direction):
                later = m + 2 if hop < NZ // 2 - 1 else NZ - 2
                next_origin = (NZ - hop - 1 if direction == 0 else hop + 1) % NZ
                remote(
                    slot, feat_slot(stage, next_origin, flip),
                    z_send.at[stage], z_recv.at[stage, direction, later], (dz, 0, 0),
                ).start()

    ticks = NZ - 1

    def tile_slot(dx, flip, i):
        return tiles_all.at[dx * 2 + flip, i]

    def send_tiles(rows):
        for n in rows:
            for i, dx, sem in ((n, 1, 0), (blocks - 1 - n, NX - 1, 1)):
                remote(
                    tiles_ref.at[i], tile_slot(NX - dx, 0, i), t_send, t_recv.at[sem, i], (0, dx, 0)
                ).start()

    def share_tiles(dx, i):
        remote(
            tile_slot(dx, 0, i), tile_slot(dx, 1, i), t_send, t_sib.at[dx, i], (0, 0, 1)
        ).start()

    def pass_tiles(rows):
        for n in rows:
            for i, dx, sem in ((n, NX - 1, 0), (blocks - 1 - n, 1, 1)):
                land(tile_slot(dx, 0, i), t_recv.at[sem, i])
                if n < blocks // 2:
                    toward = 1 if sem == 0 else NX - 1
                    remote(
                        tile_slot(dx, 0, i), tile_slot(2, 0, i), t_send, t_far.at[i], (0, toward, 0)
                    ).start()
                share_tiles(dx, i)

    near = [(0, 0, 1)] + [p for p in row if p[1] != 0] + column
    for peer in near:
        dz, dx, f = peer
        if dz == 0:
            slot = ((NX - dx) % NX) * 2 + f
        else:
            slot = 2 * NX + (NZ - dz - 1) * 2 + f
        remote(meta_ref, metas.at[slot], m_send, m_recv, peer).start()
    start_stage(0)
    for i in range(blocks):
        remote(tiles_ref.at[i], tile_slot(0, 1, i), t_send, t_sib.at[0, i], (0, 0, 1)).start()
    send_tiles(range(blocks // 2))
    own_tiles = pltpu.make_async_copy(tiles_ref, tiles_all.at[0], t_own)
    own_tiles.start()
    for f in feats:
        f[2 * NZ * blocks] = jnp.zeros((size, wide), f.dtype)
    metas[0] = meta_ref[...]

    def build_table():
        land(metas.at[pl.ds(1, len(near))], m_recv)
        copy = pltpu.make_async_copy(metas, metas_smem, m_copy)
        copy.start()
        copy.wait()

        for reader in range(2 * NX):
            dx, f = reader // 2, reader % 2
            reader_index = dom_index(my_z, lax.rem(my_x + dx, NX), other if f else core)

            def entry(n, carry):
                col = metas_smem[reader, 0, n]
                owner = jnp.maximum(col - blocks, 0)
                valid = (col >= blocks) & ((owner // 2) % NX == my_x)
                dz = (owner // (2 * NX) - my_z + NZ) % NZ
                flip = (owner + core) % 2
                where = jnp.where(dz == 0, flip, 2 * NX + (dz - 1) * 2 + flip)
                block = metas_smem[where, 1, reader_index]
                slot = (dz * 2 + flip) * blocks + block
                table[reader * blocks * slots + n] = jnp.where(valid, slot, 2 * NZ * blocks)
                return carry

            lax.fori_loop(0, blocks * slots, entry, 0)

    def partial(stage, reader):
        feat = feats[stage]

        def one(i, carry):
            first = (reader * blocks + i) * slots
            left = jnp.concatenate([tiles_all[reader, i, k] for k in range(slots)], axis=1)
            right = jnp.concatenate([feat[table[first + k]] for k in range(slots)], axis=0)
            total = jnp.dot(left, right, preferred_element_type=jnp.float32)
            part_out[stage, reader, i] = total.astype(part_out.dtype)
            return carry

        lax.fori_loop(0, blocks, one, 0)
        if reader:
            dx, f = reader // 2, reader % 2
            remote(
                part_out.at[stage, reader], part_in.at[stage, ((NX - dx) % NX) * 2 + f],
                p_send.at[stage], p_recv.at[stage], (0, dx, f),
            ).start()

    def finish(stage):
        land(part_in.at[stage, pl.ds(1, 2 * NX - 1)], p_recv.at[stage])
        for flip in range(2):
            half = other if flip else core
            for i in range(blocks):
                total = (part_in if flip else part_out)[stage, flip, i].astype(jnp.float32)
                for dx in range(1, NX):
                    total += part_in[stage, dx * 2 + flip, i].astype(jnp.float32)
                out_ref[stage // 2, half * 2 + stage % 2, i] = total

    order = (0, 1, 2, 3, 6, 7, 4, 5)
    last_order = (4, 5, 2, 3, 6, 7, 0, 1)

    def stage_ready(stage):
        land(feat_slot(stage, 0, 1), sib_recv.at[stage])
        land(feat_slot(stage, 0, 0), own_sem.at[stage])

    for stage in range(STAGES):
        for m in range(ticks):
            ring_tick(stage, m)
            if m == 2 and stage + 1 < STAGES:
                start_stage(stage + 1)
            if stage == 0:
                if m == 1:
                    send_tiles(range(blocks // 2, blocks))
                if m == 2:
                    build_table()
                if m == 5:
                    pass_tiles(range(blocks // 2))
            else:
                if stage == 1 and m == 0:
                    own_tiles.wait()
                    for i in range(blocks):
                        land(tile_slot(0, 1, i), t_sib.at[0, i])
                if stage == 1 and m == 1:
                    pass_tiles(range(blocks // 2, blocks))
                if stage == 1 and m == 2:
                    for i in range(blocks):
                        land(tile_slot(1, 1, i), t_sib.at[1, i])
                        land(tile_slot(NX - 1, 1, i), t_sib.at[NX - 1, i])
                if stage == 1 and m == 5:
                    for i in range(blocks):
                        land(tile_slot(2, 0, i), t_far.at[i])
                        share_tiles(2, i)
                if stage == 1 and m == 6:
                    for i in range(blocks):
                        land(tile_slot(2, 1, i), t_sib.at[2, i])
                partial(stage - 1, order[m])
                if m == ticks - 1:
                    partial(stage - 1, order[m + 1])
        stage_ready(stage)
    last = STAGES - 1
    for reader in last_order:
        partial(last, reader)
    for stage in range(STAGES):
        finish(stage)

    for stage in range(STAGES):
        sent = 15 * blocks
        land(feats[stage].at[pl.ds(0, sent)], z_send.at[stage])
        land(part_out.at[stage, pl.ds(1, 2 * NX - 1)], p_send.at[stage])
    for _ in range(1):
        land(metas.at[pl.ds(1, len(near))], m_send)
    land(tiles_all.at[pl.ds(1, 2 * NX - 1)], t_send)


def exchange(initial, history, tiles, meta):
    blocks, size, width = initial.shape
    slots = tiles.shape[1]
    wide = width // 4
    vmem = pl.BlockSpec(memory_space=pltpu.VMEM)
    dma = pltpu.SemaphoreType.DMA
    metas = 2 * NX + 2 * (NZ - 1)
    return pl.pallas_call(
        exchange_kernel,
        out_shape=jax.ShapeDtypeStruct((2, 4, blocks, size, wide), jnp.float32),
        in_specs=[vmem] * 4,
        out_specs=vmem,
        scratch_shapes=[pltpu.VMEM((2 * NZ * blocks + 1, size, wide), jnp.bfloat16)] * STAGES
        + [
            pltpu.VMEM((2 * NX, blocks, slots, size, size), jnp.bfloat16),
            pltpu.VMEM((STAGES, 2 * NX, blocks, size, wide), jnp.bfloat16),
            pltpu.VMEM((STAGES, 2 * NX, blocks, size, wide), jnp.bfloat16),
            pltpu.VMEM((metas, 8, 128), jnp.int32),
            pltpu.SMEM((metas, 8, 128), jnp.int32),
            pltpu.SMEM((2 * NX * blocks * slots,), jnp.int32),
            dma((STAGES, 2, NZ - 1)),
            dma((STAGES,)),
            dma((STAGES,)),
            dma((STAGES,)),
            dma((2, blocks)),
            dma((blocks,)),
            dma((NX, blocks)),
            dma,
            dma,
            dma((STAGES,)),
            dma((STAGES,)),
            dma,
            dma,
            dma,
        ],
        compiler_params=pltpu.CompilerParams(
            collective_id=0, has_side_effects=True, vmem_limit_bytes=56 * 2**20
        ),
        cost_estimate=pl.CostEstimate(
            flops=5 * 10**9, bytes_accessed=8 * 2**20, transcendentals=0
        ),
        name="exchange",
    )(initial, history, tiles, meta)


def sigmoid(value):
    return 1.0 / (1.0 + jnp.exp(-value))


def dense_kernel(
    initial_ref, tiles_ref, cols_ref, remote_ref, one_ref, two_ref, cot_ref,
    out_ref, grads_ref, local_ref,
):
    blocks, slots, size, _ = tiles_ref.shape
    width = initial_ref.shape[1]
    wide = width // 4
    f32 = jnp.float32

    def dot(a, b, dims=((1,), (0,))):
        return lax.dot_general(a, b, (dims, ((), ())), preferred_element_type=f32)

    for i in range(blocks):
        sums = [jnp.zeros((size, size), f32) for _ in range(blocks)]
        for k in range(slots):
            tile = tiles_ref[i, k].astype(f32)
            for c in range(blocks):
                mask = jnp.where(cols_ref[i, k] == c, 1.0, 0.0).astype(f32)
                sums[c] += tile * mask
        for c in range(blocks):
            local_ref[pl.ds(i * size, size), pl.ds(c * size, size)] = sums[c].astype(jnp.bfloat16)

    def received(which):
        return jnp.concatenate(
            [remote_ref[which, q].reshape(blocks * size, wide) for q in range(4)], axis=1
        )

    own = initial_ref[...]
    own_float = own.astype(f32)
    local = local_ref[...]
    mixed_one = (
        (1.0 - RESTART) * (dot(local, own) + received(0)) + RESTART * own_float
    ).astype(jnp.bfloat16)
    pre_one = (1.0 - BETA_ONE) * mixed_one.astype(f32) + BETA_ONE * dot(mixed_one, one_ref[...])
    sig_one = sigmoid(pre_one)
    hidden = (pre_one * sig_one).astype(jnp.bfloat16)
    slope_one = sig_one * (1.0 + pre_one * (1.0 - sig_one))
    mixed_two = (
        (1.0 - RESTART) * (dot(local, hidden) + received(1)) + RESTART * own_float
    ).astype(jnp.bfloat16)
    pre_two = (1.0 - BETA_TWO) * mixed_two.astype(f32) + BETA_TWO * dot(mixed_two, two_ref[...])
    sig_two = sigmoid(pre_two)
    out_ref[...] = (pre_two * sig_two).astype(jnp.bfloat16)
    slope_two = sig_two * (1.0 + pre_two * (1.0 - sig_two))
    back_two = (cot_ref[...].astype(f32) * slope_two).astype(jnp.bfloat16)
    grad_two = dot(mixed_two, back_two, ((0,), (0,)))
    back_mixed = (
        (1.0 - BETA_TWO) * back_two.astype(f32)
        + BETA_TWO * dot(back_two, two_ref[...], ((1,), (1,)))
    ).astype(jnp.bfloat16)
    back_hidden = (1.0 - RESTART) * dot(local, back_mixed, ((0,), (0,)))
    back_one = (back_hidden * slope_one).astype(jnp.bfloat16)
    grad_one = dot(mixed_one, back_one, ((0,), (0,)))
    for q in range(4):
        for g, grad in ((0, grad_one), (1, grad_two)):
            grads_ref[g, q] = grad[:, q * wide : (q + 1) * wide].astype(jnp.bfloat16)


def dense(initial, tiles, cols, received, weight_one, weight_two, cotangent):
    rows, width = initial.shape
    vmem = pl.BlockSpec(memory_space=pltpu.VMEM)
    smem = pl.BlockSpec(memory_space=pltpu.SMEM)
    return pl.pallas_call(
        dense_kernel,
        out_shape=(
            jax.ShapeDtypeStruct((rows, width), jnp.bfloat16),
            jax.ShapeDtypeStruct((2, 4, width, width // 4), jnp.bfloat16),
        ),
        in_specs=[vmem, vmem, smem, vmem, vmem, vmem, vmem],
        out_specs=(vmem, vmem),
        scratch_shapes=[pltpu.VMEM((rows, rows), jnp.bfloat16)],
        compiler_params=pltpu.CompilerParams(vmem_limit_bytes=56 * 2**20),
        cost_estimate=pl.CostEstimate(
            flops=2 * 10**9, bytes_accessed=8 * 2**20, transcendentals=2**19
        ),
        name="dense",
    )(initial, tiles, cols, received, weight_one, weight_two, cotangent)


def reduce_kernel(
    grads_ref, out_ref, pair_in, pair_sum, x_in, x_sum, far_in, done,
    pair_send, pair_recv, x_send, x_recv, far_send, far_recv,
    done_send, done_recv, gx_send, gx_recv, back_send, back_recv,
):
    f32 = jnp.float32
    dom = lax.axis_index("dom")
    my_y = lax.axis_index("grp")
    core = lax.rem(dom, 2)
    my_x = lax.rem(dom // 2, NX)
    my_z = dom // (2 * NX)
    other = 1 - core
    units = grads_ref.shape[1]
    per_x = units // NX

    def across(dx):
        return (dom_index(my_z, lax.rem(my_x + dx, NX), core), my_y)

    def plane(dz, dy):
        return (dom_index(lax.rem(my_z + dz, NZ), my_x, core), lax.rem(my_y + dy, NY))

    pair = (dom_index(my_z, my_x, other), my_y)
    spread = [(dz, dy) for dz in range(NZ) for dy in range(NY) if dz or dy]

    barrier = pltpu.get_barrier_semaphore()
    peers = [pair] + [across(dx) for dx in range(1, NX)] + [plane(*p) for p in spread]
    for peer in peers:
        pl.semaphore_signal(barrier, inc=1, device_id=peer, device_id_type=MESH)
    pl.semaphore_wait(barrier, len(peers))

    def remote(src, dst, send_sem, recv_sem, peer):
        return pltpu.make_async_remote_copy(
            src_ref=src, dst_ref=dst, send_sem=send_sem, recv_sem=recv_sem,
            device_id=peer, device_id_type=MESH,
        )

    def land(ref, sem):
        pltpu.make_async_copy(ref, ref, sem).wait()

    remote(grads_ref.at[other], pair_in, pair_send, pair_recv, pair).start()
    land(pair_in, pair_recv)
    pair_sum[...] = (grads_ref[core].astype(f32) + pair_in[...].astype(f32)).astype(pair_sum.dtype)

    for dx in range(1, NX):
        quarter = lax.rem(my_x + dx, NX)
        remote(
            pair_sum.at[pl.ds(quarter * per_x, per_x)], x_in.at[NX - dx - 1],
            x_send, x_recv, across(dx),
        ).start()
    total = pair_sum[pl.ds(my_x * per_x, per_x)].astype(f32)
    land(x_in, x_recv)
    for n in range(NX - 1):
        total += x_in[n].astype(f32)
    x_sum[...] = total.astype(x_sum.dtype)

    mine = my_z * NY + my_y
    for n, (dz, dy) in enumerate(spread):
        theirs = lax.rem(my_z + dz, NZ) * NY + lax.rem(my_y + dy, NY)
        back = ((NZ - dz) % NZ) * NY + (NY - dy) % NY - 1
        remote(
            x_sum.at[theirs], far_in.at[back], far_send, far_recv, plane(dz, dy)
        ).start()
    land(far_in, far_recv)
    unit = x_sum[mine].astype(f32)
    for n in range(len(spread)):
        unit += far_in[n].astype(f32)
    done[mine] = unit.astype(done.dtype)

    for n, (dz, dy) in enumerate(spread):
        remote(
            done.at[mine], done.at[mine], done_send, done_recv, plane(dz, dy)
        ).start()
    land(done.at[pl.ds(0, len(spread))], done_recv)
    here = pl.ds(my_x * per_x, per_x)
    for dx in range(1, NX):
        remote(done, out_ref.at[core, here], gx_send, gx_recv.at[NX - dx - 1], across(dx)).start()
    remote(done, out_ref.at[core, here], back_send, back_recv.at[0], pair).start()
    out_ref[core, here] = done[...]
    for dx in (1, NX - 1, 2):
        got = pl.ds(lax.rem(my_x + dx, NX) * per_x, per_x)
        land(out_ref.at[core, got], gx_recv.at[dx - 1])
        remote(
            out_ref.at[core, got], out_ref.at[core, got], back_send, back_recv.at[dx], pair
        ).start()
    for dx in range(NX):
        got = pl.ds(lax.rem(my_x + dx, NX) * per_x, per_x)
        land(out_ref.at[other, got], back_recv.at[dx])

    land(pair_in, pair_send)
    land(x_in, x_send)
    land(far_in, far_send)
    land(far_in, done_send)
    land(x_in, gx_send)
    land(pair_in, back_send)


def reduce_all(grads):
    _, units, rows, lanes = grads.shape
    per_x = units // NX
    vmem = pl.BlockSpec(memory_space=pltpu.VMEM)
    dma = pltpu.SemaphoreType.DMA
    bf16 = grads.dtype
    return pl.pallas_call(
        reduce_kernel,
        out_shape=jax.ShapeDtypeStruct(grads.shape, bf16),
        in_specs=[vmem],
        out_specs=vmem,
        scratch_shapes=[
            pltpu.VMEM((units, rows, lanes), bf16),
            pltpu.VMEM((units, rows, lanes), bf16),
            pltpu.VMEM((NX - 1, per_x, rows, lanes), bf16),
            pltpu.VMEM((per_x, rows, lanes), bf16),
            pltpu.VMEM((NZ * NY - 1, rows, lanes), bf16),
            pltpu.VMEM((per_x, rows, lanes), bf16),
            dma, dma, dma, dma, dma, dma, dma, dma,
            dma,
            dma((NX - 1,)),
            dma,
            dma((NX,)),
        ],
        compiler_params=pltpu.CompilerParams(
            collective_id=1, has_side_effects=True, vmem_limit_bytes=32 * 2**20
        ),
        cost_estimate=pl.CostEstimate(flops=10**6, bytes_accessed=2 * 2**20, transcendentals=0),
        name="reduce_all",
    )(grads)


def local(initial, history, tile_values, tile_cols, send_blocks, weight_one, weight_two, cotangent):
    tiles = tile_values[0]
    cols = tile_cols[0]
    blocks, slots, size, _ = tiles.shape
    width = initial.shape[2]
    meta = jnp.concatenate(
        [
            jnp.pad(cols.reshape(1, blocks * slots), ((0, 0), (0, 128 - blocks * slots))),
            jnp.pad(send_blocks[0], ((0, 0), (0, 128 - send_blocks.shape[2]))),
            jnp.zeros((6, 128), jnp.int32),
        ],
        axis=0,
    )
    received = exchange(
        initial[0].reshape(blocks, size, width), history[0].reshape(blocks, size, width), tiles, meta
    )
    output, grads = dense(initial[0], tiles, cols, received, weight_one, weight_two, cotangent[0])
    wide = width // 4
    summed = reduce_all(grads.reshape(2, 4 * width // 16, 16, wide))
    summed = summed.reshape(2, 4, width, wide).transpose(0, 2, 1, 3).reshape(2, width, width)
    grad_one = BETA_ONE * summed[0].astype(jnp.float32)
    grad_two = BETA_TWO * summed[1].astype(jnp.float32)
    return (output[None], grad_one, grad_two)


def solution(mesh):
    return jax.shard_map(
        local,
        mesh=mesh,
        in_specs=(
            P("grp", "dom", None),
            P("grp", "dom", None),
            P("grp", "dom", None, None, None),
            P("grp", "dom", None),
            P("grp", "dom", None),
            P(),
            P(),
            P("grp", "dom", None),
        ),
        out_specs=(P("grp", "dom", None), P(), P()),
        check_vma=False,
    )
```

time: 756 us -> 180 us (0.24)
  waiting for transfers between devices: 641 us -> 0 us
  Pallas kernels: 0 us -> 173 us
  local copies, waits for them, and re-layouts: 31 us -> 4.91 us
  starting transfers between devices: 23.4 us -> 0 us
  other arithmetic: 20 us -> 1.49 us
  matrix products: 16.5 us -> 0 us
  between operations: 14.1 us -> 0.67 us
  loops' own time: 7.61 us -> 0 us
    all_to_all x2 -> x0, waiting for transfers between devices: 337 us -> none  [the longest x1 177 us: local(): lax.all_to_all(outgoing_in, 'dom', split_axis=0, concat_axis=0, tiled=True)]
    psum x1 -> x0, waiting for transfers between devices: 304 us -> none  [local(): grad_one, grad_two = lax.psum((grad_one, grad_two), ('dom', 'grp'))]
    pallas_call x0 -> x3, Pallas kernels: none -> 173 us  [the longest x1 128 us: exchange(): pl.pallas_call(exchange_kernel, out_shape=jax.ShapeDtypeStruct((2, 4, blo...]
    gather x4 -> x0, local copies, waits for them, and re-layouts: 24.8 us -> none  [the longest x2 12.8 us: propagate(): picked = buffer[col_part]]
    all_to_all x2 -> x0, starting transfers between devices: 23.4 us -> none  [the longest x1 13.1 us: local(): lax.all_to_all(outgoing_in, 'dom', split_axis=0, concat_axis=0, tiled=True)]
    dot_general x8 -> x0, matrix products: 16.5 us -> none  [the longest x2 5.92 us: propagate(): jnp.einsum('rkij,rkjd->rid', tile_part, picked, preferred_element_type=jn...]
    concatenate x2 -> x1, other arithmetic: 15.2 us -> 1.32 us  [local(): jnp.concatenate([jnp.pad(cols.reshape(1, blocks * slots), ((0, 0), (0, 12...]
    another operation x1 -> x0, loops' own time: 7.61 us -> none  [local_transpose(): return lax.fori_loop(0, local_count, add_tile, start)]
  transfers between devices with their start and end apart: 3 -> 0, of which waited for: 3 -> 0; matrix products, arithmetic and copies ran while one was open for 4% -> 0% of each run, Pallas kernels for 0% -> 0%
where the time goes in v1:
time: 180 us
  Pallas kernels  173 us (96%)
  local copies, waits for them, and re-layouts  4.91 us (3%)
    pallas_call x1, Pallas kernels, exchange(): pl.pallas_call(exchange_kernel, out_shape=jax.ShapeDtypeStruct((2, 4, blo...  128 us
    pallas_call x1, Pallas kernels, reduce_all(): pl.pallas_call(reduce_kernel, out_shape=jax.ShapeDtypeStruct(grads.shape,...  38.3 us
    pallas_call x1, Pallas kernels, dense(): pl.pallas_call(dense_kernel, out_shape=(jax.ShapeDtypeStruct((rows, width...  7.16 us

profile of v1, /device:TPU:1, one launch (start us, length us, event | category | flops | bytes accessed | tf_op | source)
XLA Modules:
  0.0 180.2 jit_solution(6544666708461769029)
XLA Ops:
  0.6 0.8 reshape_squeeze.11
  1.4 0.1 pad.12.clone
  1.5 1.3 fusion.meta_ref
  2.8 127.7 %exchange.1.remote_ref = f32[2,4,4,128,128]{4,3,2,1,0:T(8,128)} custom-call(bf16[4,128,512]{2,1,0:T(8,128)(2,1)} %bitcast.29, bf16[4,128,512]{2,1,0:T(8,128)(2,1)} %bitcast.28, bf16[4,8,128,128]{3,2,1,0:T(8,128)(2,1)} %bitcast.26, s32[8,128]{1,0:T(8,128)} %fusion.meta_ref), custom_call_target="tpu_custom_call" | custom-call | flops 5000000000 | bytes 8388608 | tf_op jit(solution)/shard_map/exchange/pallas_call | solution.py:261
  130.5 7.2 %dense.1 = (bf16[512,512]{1,0:T(8,128)(2,1)}, bf16[2,4,512,128]{3,2,1,0:T(8,128)(2,1)}) custom-call(bf16[512,512]{1,0:T(8,128)(2,1)} %bitcast.30, bf16[4,8,128,128]{3,2,1,0:T(8,128)(2,1)} %bitcast.27, s32[4,8]{1,0:T(4,128)} %bitcast.24, f32[2,4,4,128,128]{4,3,2,1,0:T(8,128)} %exchange.1.remote_ref, bf16[512,512]{1,0:T(8,128)(2,1)} %one_ref.1, ...), custom_call_target="tpu_custom_call" | custom-call | flops 2000000000 | bytes 8388608 | tf_op jit(solution)/shard_map/dense/pallas_call | solution.py:365
  137.7 0.0 copy-start
  137.7 1.2 copy-done
  138.9 38.3 %reduce_all.1 = bf16[2,128,16,128]{3,2,1,0:T(8,128)(2,1)S(1)} custom-call(bf16[2,128,16,128]{3,2,1,0:T(8,128)(2,1)S(1)} %bitcast.21), custom_call_target="tpu_custom_call" | custom-call | flops 1000000 | bytes 2097152 | tf_op jit(solution)/shard_map/reduce_all/pallas_call | solution.py:484
  177.2 0.2 convert_multiply_fusion
  177.4 0.7 copy.12
  178.1 0.7 copy.11
  178.8 1.5 copy_bitcast_fusion
  (1 shorter events, 0.0 us)
Async XLA Ops:
  137.7 1.2 copy-start

commit v2 on v0

v2 whole, which is shorter than its diff:
```python
import functools

import jax
import jax.numpy as jnp
from jax import lax
from jax.experimental import pallas as pl
from jax.experimental.pallas import tpu as pltpu
from jax.sharding import PartitionSpec as P

RESTART = 0.1
BETA_ONE = 0.405465
BETA_TWO = 0.223144

NZ = 8
NX = 4
NY = 4
STAGES = 4
MESH = pl.DeviceIdType.MESH


def dom_index(z, x, core):
    return (z * NX + x) * 2 + core


def sigmoid(value):
    return 1.0 / (1.0 + jnp.exp(-value))


def dot(a, b, dims=((1,), (0,))):
    return lax.dot_general(a, b, (dims, ((), ())), preferred_element_type=jnp.float32)


def layers_kernel(
    initial_ref, history_ref, tiles_ref, cols_ref, chosen_ref, one_ref, two_ref, cot_ref,
    out_ref, sum_ref,
    feat0, feat1, feat2, feat3, tiles_all, part_out, part_in, relay_in, metas, metas_smem, table,
    local_ref, base_ref, received_ref, mixed_one_ref, mixed_two_ref, hidden_ref, slope_ref,
    grad_ref, send_ref, pair_in, pair_sum, first_in, first_sum, first_out, second_in,
    third, third_in, third_done,
    z_recv, sib_recv, z_send, own_sem, t_recv, t_far, t_sib, t_send, t_own, p_recv, p_send,
    relay_recv, relay_send, m_recv, m_send, m_copy, pair_sems, first_send, first_recv,
    second_send, second_recv, third_send, third_recv, done_send, done_recv,
    gather_send, gather_recv, share_send, share_recv, back_send, back_recv,
):
    f32 = jnp.float32
    bf16 = jnp.bfloat16
    feats = (feat0, feat1, feat2, feat3)
    blocks, size, width = initial_ref.shape
    slots = tiles_ref.shape[1]
    wide = feat0.shape[2]
    rows = blocks * size
    dom = lax.axis_index("dom")
    my_y = lax.axis_index("grp")
    core = lax.rem(dom, 2)
    my_x = lax.rem(dom // 2, NX)
    my_z = dom // (2 * NX)
    other = 1 - core

    def at(dz, dx, flip, dy=0):
        z = lax.rem(my_z + dz, NZ)
        x = lax.rem(my_x + dx, NX)
        y = lax.rem(my_y + dy, NY)
        return (dom_index(z, x, other if flip else core), y)

    row = [(0, dx, f) for dx in range(NX) for f in range(2) if (dx, f) != (0, 0)]
    column = [(dz, 0, f) for dz in range(1, NZ) for f in range(2)]
    stack = [(0, 0, 0, dy) for dy in range(1, NY)]
    barrier = pltpu.get_barrier_semaphore()
    for peer in row + column + stack:
        pl.semaphore_signal(barrier, inc=1, device_id=at(*peer), device_id_type=MESH)
    pl.semaphore_wait(barrier, len(row) + len(column) + len(stack))

    def remote(src, dst, send_sem, recv_sem, peer):
        return pltpu.make_async_remote_copy(
            src_ref=src, dst_ref=dst, send_sem=send_sem, recv_sem=recv_sem,
            device_id=at(*peer), device_id_type=MESH,
        )

    def land(ref, sem):
        pltpu.make_async_copy(ref, ref, sem).wait()

    def feat_slot(stage, dz, flip):
        return feats[stage].at[pl.ds((dz * 2 + flip) * blocks, blocks)]

    def own_columns(stage, flip):
        ref = (initial_ref, history_ref)[stage // 2]
        half = other if flip else core
        start = pl.multiple_of((half * 2 + stage % 2) * wide, wide)
        return ref.at[:, :, pl.ds(start, wide)]

    def start_stage(stage):
        for flip in range(2):
            for direction, dz in ((0, 1), (1, NZ - 1)):
                remote(
                    own_columns(stage, flip), feat_slot(stage, NZ - dz, flip),
                    z_send.at[stage], z_recv.at[stage, direction, flip], (dz, 0, flip),
                ).start()
        remote(
            own_columns(stage, 1), feat_slot(stage, 0, 1),
            z_send.at[stage], sib_recv.at[stage], (0, 0, 1),
        ).start()
        pltpu.make_async_copy(own_columns(stage, 0), feat_slot(stage, 0, 0), own_sem.at[stage]).start()

    def ring_tick(stage, m):
        for direction, dz in ((0, 1), (1, NZ - 1)):
            hop = m // 2 + 1
            flip = m % 2 if hop < NZ // 2 else direction
            origin = (NZ - hop if direction == 0 else hop) % NZ
            slot = feat_slot(stage, origin, flip)
            land(slot, z_recv.at[stage, direction, m])
            if hop < NZ // 2 - 1 or (hop == NZ // 2 - 1 and flip == direction):
                later = m + 2 if hop < NZ // 2 - 1 else NZ - 2
                next_origin = (NZ - hop - 1 if direction == 0 else hop + 1) % NZ
                remote(
                    slot, feat_slot(stage, next_origin, flip),
                    z_send.at[stage], z_recv.at[stage, direction, later], (dz, 0, 0),
                ).start()

    def tile_slot(dx, flip, i):
        return tiles_all.at[dx * 2 + flip, i]

    def send_tiles(which):
        for n in which:
            for i, dx, sem in ((n, 1, 0), (blocks - 1 - n, NX - 1, 1)):
                remote(
                    tiles_ref.at[i], tile_slot(NX - dx, 0, i), t_send, t_recv.at[sem, i], (0, dx, 0)
                ).start()

    def share_tiles(dx, i):
        remote(
            tile_slot(dx, 0, i), tile_slot(dx, 1, i), t_send, t_sib.at[dx, i], (0, 0, 1)
        ).start()

    def pass_tiles(which):
        for n in which:
            for i, dx, sem in ((n, NX - 1, 0), (blocks - 1 - n, 1, 1)):
                land(tile_slot(dx, 0, i), t_recv.at[sem, i])
                if n < blocks // 2:
                    toward = 1 if sem == 0 else NX - 1
                    remote(
                        tile_slot(dx, 0, i), tile_slot(2, 0, i), t_send, t_far.at[i], (0, toward, 0)
                    ).start()
                share_tiles(dx, i)

    near = [(0, 0, 1)] + [p for p in row if p[1] != 0] + column
    metas[0, pl.ds(0, blocks), pl.ds(0, slots)] = cols_ref[...]
    metas[0, pl.ds(blocks, 1), pl.ds(0, chosen_ref.shape[1])] = chosen_ref[...]
    start_stage(0)
    for peer in near:
        dz, dx, f = peer
        if dz == 0:
            slot = ((NX - dx) % NX) * 2 + f
        else:
            slot = 2 * NX + (NZ - dz - 1) * 2 + f
        remote(metas.at[0], metas.at[slot], m_send, m_recv, peer).start()
    for i in range(blocks):
        remote(tiles_ref.at[i], tile_slot(0, 1, i), t_send, t_sib.at[0, i], (0, 0, 1)).start()
    send_tiles(range(blocks // 2))
    own_tiles = pltpu.make_async_copy(tiles_ref, tiles_all.at[0], t_own)
    own_tiles.start()
    for f in feats:
        f[2 * NZ * blocks] = jnp.zeros((size, wide), f.dtype)

    def copy_metas():
        land(metas.at[pl.ds(1, len(near))], m_recv)
        copy = pltpu.make_async_copy(metas, metas_smem, m_copy)
        copy.start()
        copy.wait()

    def build_table(readers):
        for reader in readers:
            dx, f = reader // 2, reader % 2
            reader_index = dom_index(my_z, lax.rem(my_x + dx, NX), other if f else core)

            def entry(n, carry):
                col = metas_smem[reader, n // slots, n % slots]
                owner = jnp.maximum(col - blocks, 0)
                valid = (col >= blocks) & ((owner // 2) % NX == my_x)
                dz = (owner // (2 * NX) - my_z + NZ) % NZ
                flip = (owner + core) % 2
                where = jnp.where(dz == 0, flip, 2 * NX + (dz - 1) * 2 + flip)
                block = metas_smem[where, blocks, reader_index]
                slot = (dz * 2 + flip) * blocks + block
                table[reader * blocks * slots + n] = jnp.where(valid, slot, 2 * NZ * blocks)
                return carry

            lax.fori_loop(0, blocks * slots, entry, 0)

    def build_local(i):
        sums = [jnp.zeros((size, size), f32) for _ in range(blocks)]
        for k in range(slots):
            tile = tiles_ref[i, k].astype(f32)
            for c in range(blocks):
                mask = jnp.where(metas_smem[0, i, k] == c, 1.0, 0.0).astype(f32)
                sums[c] += tile * mask
        for c in range(blocks):
            local_ref[pl.ds(i * size, size), pl.ds(c * size, size)] = sums[c].astype(bf16)

    def partial(stage, reader):
        feat = feats[stage]
        last = stage == STAGES - 1
        dx, f = reader // 2, reader % 2
        relays = (dx, f) in ((1, 0), (NX - 1, 1))
        if relays and not last:
            land(relay_in.at[stage, f], relay_recv.at[stage, f, 0])

        def send(which):
            if dx == 2:
                toward = 1 if f == 0 else NX - 1
                remote(
                    part_out.at[stage, reader, which], relay_in.at[stage, f, which],
                    relay_send.at[stage], relay_recv.at[stage, f, which if last else 0],
                    (0, toward, 0),
                ).start()
            elif reader:
                source = {0: 0, 1: 2, NX - 1: 1}[dx]
                remote(
                    part_out.at[stage, reader, which], part_in.at[stage, source * 2 + f, which],
                    p_send.at[stage], p_recv.at[stage], (0, dx, f),
                ).start()

        def one(i, carry):
            first = (reader * blocks + i) * slots
            left = jnp.concatenate([tiles_all[reader, i, k] for k in range(slots)], axis=1)
            right = jnp.concatenate([feat[table[first + k]] for k in range(slots)], axis=0)
            total = dot(left, right)
            if relays:
                if last:
                    land(relay_in.at[stage, f, i], relay_recv.at[stage, f, i])
                total += relay_in[stage, f, i].astype(f32)
            part_out[stage, reader, i] = total.astype(bf16)
            if last:
                send(i)
            return carry

        if last:
            for i in range(blocks):
                one(i, 0)
        else:
            lax.fori_loop(0, blocks, one, 0)
            send(slice(None))

    def column_chunk(stage, flip):
        return (other if flip else core) * 2 + stage % 2

    def total_of(stage, flip):
        first = part_in[stage, 1] if flip else part_out[stage, 0]
        total = first.astype(f32)
        for source in (1, 2):
            total += part_in[stage, source * 2 + flip].astype(f32)
        return total.reshape(rows, wide)

    def received(stage):
        land(part_in.at[stage, pl.ds(1, 5)], p_recv.at[stage])

    def finish_one(stage):
        received(stage)
        for flip in range(2):
            received_ref[column_chunk(stage, flip)] = total_of(stage, flip)

    def layer_one(i):
        here = pl.ds(i * size, size)
        local = local_ref[here, :]
        own = initial_ref[...].reshape(rows, width)
        got = jnp.concatenate([received_ref[q, here, :] for q in range(4)], axis=1)
        mixed = (
            (1.0 - RESTART) * (dot(local, own) + got) + RESTART * initial_ref[i].astype(f32)
        ).astype(bf16)
        pre = (1.0 - BETA_ONE) * mixed.astype(f32) + BETA_ONE * dot(mixed, one_ref[...])
        sig = sigmoid(pre)
        mixed_one_ref[here, :] = mixed
        hidden_ref[here, :] = (pre * sig).astype(bf16)
        slope_ref[here, :] = sig * (1.0 + pre * (1.0 - sig))

    def start_two():
        total = (1.0 - RESTART) * dot(local_ref[...], hidden_ref[...]) + RESTART * initial_ref[
            ...
        ].reshape(rows, width).astype(f32)
        for q in range(4):
            base_ref[q] = total[:, q * wide : (q + 1) * wide]

    def finish_two(stage):
        received(stage)
        for flip in range(2):
            chunk = column_chunk(stage, flip)
            mixed = base_ref[chunk] + (1.0 - RESTART) * total_of(stage, flip)
            mixed_two_ref[:, pl.ds(pl.multiple_of(chunk * wide, wide), wide)] = mixed.astype(bf16)

    def store_grad(g, grad):
        grad_ref[g] = grad
        send_ref[g] = grad.astype(bf16)

    def layer_two():
        mixed_two = mixed_two_ref[...]
        pre_two = (1.0 - BETA_TWO) * mixed_two.astype(f32) + BETA_TWO * dot(mixed_two, two_ref[...])
        sig = sigmoid(pre_two)
        out_ref[...] = (pre_two * sig).astype(bf16)
        slope_two = sig * (1.0 + pre_two * (1.0 - sig))
        back_two = (cot_ref[...].astype(f32) * slope_two).astype(bf16)
        back_mixed = (
            (1.0 - BETA_TWO) * back_two.astype(f32)
            + BETA_TWO * dot(back_two, two_ref[...], ((1,), (1,)))
        ).astype(bf16)
        back_hidden = (1.0 - RESTART) * dot(local_ref[...], back_mixed, ((0,), (0,)))
        back_one = (back_hidden * slope_ref[...]).astype(bf16)
        store_grad(1, dot(mixed_two, back_two, ((0,), (0,))))
        store_grad(0, dot(mixed_one_ref[...], back_one, ((0,), (0,))))

    order = [(2, 0), (2, 1), (1, 1), (3, 0), (1, 0), (3, 1), (0, 1), (0, 0)]
    first_order = [(0, 1), (0, 0), (1, 1), (3, 0), (2, 0), (2, 1), (1, 0), (3, 1)]

    for stage in range(STAGES):
        for m in range(NZ - 1):
            ring_tick(stage, m)
            if m == 2 and stage + 1 < STAGES:
                start_stage(stage + 1)
            if stage == 0:
                if m == 1:
                    send_tiles(range(blocks // 2, blocks))
                    copy_metas()
                if m >= 2 and m < 6:
                    build_table((2 * (m - 2), 2 * (m - 2) + 1))
                    build_local(m - 2)
                if m == 5:
                    pass_tiles(range(blocks // 2))
                continue
            if stage == 1:
                if m == 0:
                    own_tiles.wait()
                    for i in range(blocks):
                        land(tile_slot(0, 1, i), t_sib.at[0, i])
                if m == 1:
                    pass_tiles(range(blocks // 2, blocks))
                if m == 2:
                    for i in range(blocks):
                        land(tile_slot(1, 1, i), t_sib.at[1, i])
                        land(tile_slot(NX - 1, 1, i), t_sib.at[NX - 1, i])
                if m == 4:
                    for i in range(blocks):
                        land(tile_slot(2, 0, i), t_far.at[i])
                        share_tiles(2, i)
                if m == 5:
                    for i in range(blocks):
                        land(tile_slot(2, 1, i), t_sib.at[2, i])
            turns = [m] if m < NZ - 2 else [m, m + 1]
            for turn in turns:
                dx, f = (first_order if stage == 1 else order)[turn]
                partial(stage - 1, dx * 2 + f)
            if stage == STAGES - 1:
                if m == 0:
                    finish_one(0)
                if m == 2:
                    finish_one(1)
                if m >= 3:
                    layer_one(m - 3)
        land(feat_slot(stage, 0, 1), sib_recv.at[stage])
        land(feat_slot(stage, 0, 0), own_sem.at[stage])
    for dx, f in order:
        partial(STAGES - 1, dx * 2 + f)
    start_two()
    finish_two(2)
    finish_two(3)
    layer_two()

    remote(send_ref.at[other], pair_in, pair_sems.at[0], pair_sems.at[1], (0, 0, 1)).start()
    land(pair_in, pair_sems.at[1])
    pair_sum[...] = (grad_ref[core] + pair_in[...].astype(f32)).astype(bf16)

    half = width // 2
    quarter = half // NX
    part = quarter // NX
    place = ((my_x, my_y), (my_y, my_x))

    def rows_at(start, count):
        return pl.ds(pl.multiple_of(start, part), count)

    def along(h, turn, d):
        return (0, d, 0) if h == turn else (0, 0, 0, d)

    for d in (2, 1, 3):
        for h in range(2):
            theirs = rows_at(h * half + lax.rem(place[h][0] + d, NX) * quarter, quarter)
            remote(
                pair_sum.at[theirs], first_in.at[h, NX - d - 1],
                first_send, first_recv.at[h], along(h, 0, d),
            ).start()
    for h in range(2):
        mine = rows_at(h * half + place[h][0] * quarter, quarter)
        value = grad_ref[core, mine, :] + pair_in[mine, :].astype(f32)
        land(first_in.at[h], first_recv.at[h])
        for n in range(NX - 1):
            value += first_in[h, n].astype(f32)
        first_sum[h] = value
        first_out[h] = value.astype(bf16)
        for d in (2, 1, 3):
            theirs = rows_at(lax.rem(place[h][1] + d, NX) * part, part)
            remote(
                first_out.at[h, theirs], second_in.at[h, NX - d - 1],
                second_send, second_recv.at[h], along(h, 1, d),
            ).start()
    tiles_of = [(r, q) for r in range(part // 8) for q in range(4)]
    for h in range(2):
        value = first_sum[h, rows_at(place[h][1] * part, part), :]
        land(second_in.at[h], second_recv.at[h])
        for n in range(NX - 1):
            value += second_in[h, n].astype(f32)
        for n, (r, q) in enumerate(tiles_of):
            third[h, n] = value[r * 8 : (r + 1) * 8, q * wide : (q + 1) * wide]
        for dz in range(1, NZ):
            remote(
                third.at[h, lax.rem(my_z + dz, NZ)], third_in.at[h, NZ - dz - 1],
                third_send, third_recv.at[h], (dz, 0, 0),
            ).start()
    for h in range(2):
        value = third[h, my_z]
        land(third_in.at[h], third_recv.at[h])
        for n in range(NZ - 1):
            value += third_in[h, n]
        third_done[h, my_z] = value
        for dz in range(1, NZ):
            remote(
                third_done.at[h, my_z], third_done.at[h, my_z],
                done_send, done_recv.at[h], (dz, 0, 0),
            ).start()

    for h in range(2):
        land(third_done.at[h, pl.ds(0, NZ - 1)], done_recv.at[h])
        value = jnp.concatenate(
            [
                jnp.concatenate([third_done[h, r * 4 + q] for q in range(4)], axis=1)
                for r in range(part // 8)
            ],
            axis=0,
        )
        mine = rows_at(h * half + place[h][0] * quarter + place[h][1] * part, part)
        sum_ref[core, mine, :] = value.astype(bf16)
        for d in (2, 1, 3):
            remote(
                sum_ref.at[core, mine], sum_ref.at[core, mine],
                gather_send, gather_recv.at[h], along(h, 1, d),
            ).start()
    for h in range(2):
        land(second_in.at[h], gather_recv.at[h])
        mine = rows_at(h * half + place[h][0] * quarter, quarter)
        for d in (2, 1, 3):
            remote(
                sum_ref.at[core, mine], sum_ref.at[core, mine],
                share_send, share_recv.at[h, NX - d - 1], along(h, 0, d),
            ).start()
        remote(
            sum_ref.at[core, mine], sum_ref.at[core, mine],
            back_send, back_recv.at[h, 0], (0, 0, 1),
        ).start()

    def share_at(h, d):
        return rows_at(h * half + lax.rem(place[h][0] + d, NX) * quarter, quarter)

    for d in (1, 3, 2):
        for h in range(2):
            got = share_at(h, d)
            land(sum_ref.at[core, got], share_recv.at[h, d - 1])
            remote(
                sum_ref.at[core, got], sum_ref.at[core, got],
                back_send, back_recv.at[h, d], (0, 0, 1),
            ).start()
    for d in range(NX):
        for h in range(2):
            land(sum_ref.at[other, share_at(h, d)], back_recv.at[h, d])

    for stage in range(STAGES):
        land(feats[stage].at[pl.ds(0, 15 * blocks)], z_send.at[stage])
        land(part_in.at[stage, pl.ds(1, 5)], p_send.at[stage])
        land(relay_in.at[stage], relay_send.at[stage])
    land(metas.at[pl.ds(1, len(near))], m_send)
    land(tiles_all.at[pl.ds(1, 2 * NX - 1)], t_send)
    land(pair_in, pair_sems.at[0])
    land(first_in, first_send)
    land(second_in, second_send)
    land(third_in, third_send)
    land(third_in, done_send)
    land(second_in, gather_send)
    land(first_in, share_send)
    land(pair_in, back_send)


def layers(initial, history, tiles, cols, chosen, weight_one, weight_two, cotangent):
    blocks, size, width = initial.shape
    slots = tiles.shape[1]
    wide = width // 4
    rows = blocks * size
    quarter = width // 2 // NX
    part = quarter // NX
    vmem = pl.BlockSpec(memory_space=pltpu.VMEM)
    dma = pltpu.SemaphoreType.DMA
    bf16 = jnp.bfloat16
    f32 = jnp.float32
    metas = 2 * NX + 2 * (NZ - 1)
    return pl.pallas_call(
        layers_kernel,
        out_shape=(
            jax.ShapeDtypeStruct((rows, width), bf16),
            jax.ShapeDtypeStruct((2, width, width), bf16),
        ),
        in_specs=[vmem] * 8,
        out_specs=(vmem, vmem),
        scratch_shapes=[pltpu.VMEM((2 * NZ * blocks + 1, size, wide), bf16)] * STAGES
        + [
            pltpu.VMEM((2 * NX, blocks, slots, size, size), bf16),
            pltpu.VMEM((STAGES, 2 * NX, blocks, size, wide), bf16),
            pltpu.VMEM((STAGES, 6, blocks, size, wide), bf16),
            pltpu.VMEM((STAGES, 2, blocks, size, wide), bf16),
            pltpu.VMEM((metas, 8, 128), jnp.int32),
            pltpu.SMEM((metas, 8, 128), jnp.int32),
            pltpu.SMEM((2 * NX * blocks * slots,), jnp.int32),
            pltpu.VMEM((rows, rows), bf16),
            pltpu.VMEM((4, rows, wide), f32),
            pltpu.VMEM((4, rows, wide), f32),
            pltpu.VMEM((rows, width), bf16),
            pltpu.VMEM((rows, width), bf16),
            pltpu.VMEM((rows, width), bf16),
            pltpu.VMEM((rows, width), f32),
            pltpu.VMEM((2, width, width), f32),
            pltpu.VMEM((2, width, width), bf16),
            pltpu.VMEM((width, width), bf16),
            pltpu.VMEM((width, width), bf16),
            pltpu.VMEM((2, NX - 1, quarter, width), bf16),
            pltpu.VMEM((2, quarter, width), f32),
            pltpu.VMEM((2, quarter, width), bf16),
            pltpu.VMEM((2, NX - 1, part, width), bf16),
            pltpu.VMEM((2, NZ, 8, wide), f32),
            pltpu.VMEM((2, NZ - 1, 8, wide), f32),
            pltpu.VMEM((2, NZ, 8, wide), f32),
            dma((STAGES, 2, NZ - 1)),
            dma((STAGES,)),
            dma((STAGES,)),
            dma((STAGES,)),
            dma((2, blocks)),
            dma((blocks,)),
            dma((NX, blocks)),
            dma,
            dma,
            dma((STAGES,)),
            dma((STAGES,)),
            dma((STAGES, 2, blocks)),
            dma((STAGES,)),
            dma,
            dma,
            dma,
            dma((2,)),
            dma,
            dma((2,)),
            dma,
            dma((2,)),
            dma,
            dma((2,)),
            dma,
            dma((2,)),
            dma,
            dma((2,)),
            dma,
            dma((2, NX - 1)),
            dma,
            dma((2, NX)),
        ],
        compiler_params=pltpu.CompilerParams(
            collective_id=0, has_side_effects=True, vmem_limit_bytes=56 * 2**20
        ),
        cost_estimate=pl.CostEstimate(
            flops=7 * 10**9, bytes_accessed=8 * 2**20, transcendentals=2**19
        ),
        name="layers",
    )(initial, history, tiles, cols, chosen, weight_one, weight_two, cotangent)


def local(initial, history, tile_values, tile_cols, send_blocks, weight_one, weight_two, cotangent):
    tiles = tile_values[0]
    blocks, slots, size, _ = tiles.shape
    width = initial.shape[2]
    output, summed = layers(
        initial[0].reshape(blocks, size, width), history[0].reshape(blocks, size, width),
        tiles, tile_cols[0], send_blocks[0], weight_one, weight_two, cotangent[0],
    )
    grad_one = BETA_ONE * summed[0].astype(jnp.float32)
    grad_two = BETA_TWO * summed[1].astype(jnp.float32)
    return (output[None], grad_one, grad_two)


def solution(mesh):
    return jax.shard_map(
        local,
        mesh=mesh,
        in_specs=(
            P("grp", "dom", None),
            P("grp", "dom", None),
            P("grp", "dom", None, None, None),
            P("grp", "dom", None),
            P("grp", "dom", None),
            P(),
            P(),
            P("grp", "dom", None),
        ),
        out_specs=(P("grp", "dom", None), P(), P()),
        check_vma=False,
    )
```

time: 756 us -> 160 us (0.21)
  waiting for transfers between devices: 641 us -> 0 us
  Pallas kernels: 0 us -> 156 us
  local copies, waits for them, and re-layouts: 31 us -> 0.8 us
  starting transfers between devices: 23.4 us -> 0 us
  other arithmetic: 20 us -> 2.87 us
  matrix products: 16.5 us -> 0 us
  between operations: 14.1 us -> 0.65 us
  loops' own time: 7.61 us -> 0 us
    all_to_all x2 -> x0, waiting for transfers between devices: 337 us -> none  [the longest x1 177 us: local(): lax.all_to_all(outgoing_in, 'dom', split_axis=0, concat_axis=0, tiled=True)]
    psum x1 -> x0, waiting for transfers between devices: 304 us -> none  [local(): grad_one, grad_two = lax.psum((grad_one, grad_two), ('dom', 'grp'))]
    pallas_call x0 -> x1, Pallas kernels: none -> 156 us  [layers(): pl.pallas_call(layers_kernel, out_shape=(jax.ShapeDtypeStruct((rows, widt...]
    gather x4 -> x0, local copies, waits for them, and re-layouts: 24.8 us -> none  [the longest x2 12.8 us: propagate(): picked = buffer[col_part]]
    all_to_all x2 -> x0, starting transfers between devices: 23.4 us -> none  [the longest x1 13.1 us: local(): lax.all_to_all(outgoing_in, 'dom', split_axis=0, concat_axis=0, tiled=True)]
    dot_general x8 -> x0, matrix products: 16.5 us -> none  [the longest x2 5.92 us: propagate(): jnp.einsum('rkij,rkjd->rid', tile_part, picked, preferred_element_type=jn...]
    concatenate x2 -> x0, other arithmetic: 15.2 us -> none  [propagate(): buffer = jnp.concatenate([own_blocks, received], axis=0)]
    another operation x1 -> x0, loops' own time: 7.61 us -> none  [local_transpose(): return lax.fori_loop(0, local_count, add_tile, start)]
  transfers between devices with their start and end apart: 3 -> 0, of which waited for: 3 -> 0; matrix products, arithmetic and copies ran while one was open for 4% -> 0% of each run, Pallas kernels for 0% -> 0%
where the time goes in v2:
time: 160 us
  Pallas kernels  156 us (98%)
  other arithmetic  2.87 us (2%)
    pallas_call x1, Pallas kernels, layers(): pl.pallas_call(layers_kernel, out_shape=(jax.ShapeDtypeStruct((rows, widt...  156 us

profile of v2, /device:TPU:1, one launch (start us, length us, event | category | flops | bytes accessed | tf_op | source)
XLA Modules:
  0.0 160.3 jit_solution(2103314294883436762)
XLA Ops:
  0.6 156.0 %layers.1 = (bf16[512,512]{1,0:T(8,128)(2,1)}, bf16[2,512,512]{2,1,0:T(8,128)(2,1)}) custom-call(bf16[4,128,512]{2,1,0:T(8,128)(2,1)} %bitcast.13, bf16[4,128,512]{2,1,0:T(8,128)(2,1)} %bitcast.14, bf16[4,8,128,128]{3,2,1,0:T(8,128)(2,1)} %bitcast.12, s32[4,8]{1,0:T(4,128)} %bitcast.16, s32[1,64]{1,0:T(1,128)} %bitcast.17, bf16[512,512]{1,0:T(8,128)(2,1)} %one_ref.1, ...), custom_call_target="tpu_custom_call" | custom-call | flops 7000000000 | bytes 8388608 | tf_op jit(solution)/shard_map/layers/pallas_call | solution.py:498
  156.7 0.0 copy-start
  156.7 2.9 %multiply_bitcast_fusion = (f32[512,512]{1,0:T(8,128)}, f32[512,512]{1,0:T(8,128)}) fusion(bf16[2,512,512]{2,1,0:T(8,128)(2,1)} %get-tuple-element.6), kind=kLoop, calls=%fused_computation | loop fusion | flops 1048576 | bytes 3145728 | tf_op jit(solution)/shard_map/mul | solution.py:584
  159.5 0.0 copy-done
  159.5 0.8 copy.12
Async XLA Ops:
  156.7 2.9 %copy-start = (bf16[512,512]{1,0:T(8,128)(2,1)S(1)}, bf16[512,512]{1,0:T(8,128)(2,1)}, u32[]{:S(2)}) copy-start(bf16[512,512]{1,0:T(8,128)(2,1)} %get-tuple-element.5) | copy-start | bytes 1572868

commit v3 on v2

--- a/solution.py
+++ b/solution.py
@@ -33,7 +33,7 @@
 def layers_kernel(
     initial_ref, history_ref, tiles_ref, cols_ref, chosen_ref, one_ref, two_ref, cot_ref,
     out_ref, sum_ref,
-    feat0, feat1, feat2, feat3, tiles_all, part_out, part_in, relay_in, metas, metas_smem, table,
+    feat0, feat1, feat2, feat3, tiles_all, part_out, part_in, relay_in, relay_sum, metas, metas_smem, table,
     local_ref, base_ref, received_ref, mixed_one_ref, mixed_two_ref, hidden_ref, slope_ref,
     grad_ref, send_ref, pair_in, pair_sum, first_in, first_sum, first_out, second_in,
     third, third_in, third_done,
@@ -196,49 +196,70 @@
         for c in range(blocks):
             local_ref[pl.ds(i * size, size), pl.ds(c * size, size)] = sums[c].astype(bf16)
 
+    def product(stage, reader, i):
+        first = (reader * blocks + i) * slots
+        left = jnp.concatenate([tiles_all[reader, i, k] for k in range(slots)], axis=1)
+        right = jnp.concatenate([feats[stage][table[first + k]] for k in range(slots)], axis=0)
+        return dot(left, right)
+
+    def send_part(stage, reader, which=slice(None)):
+        dx, f = reader // 2, reader % 2
+        if dx == 2:
+            toward = 1 if f == 0 else NX - 1
+            remote(
+                part_out.at[stage, reader, which], relay_in.at[stage, f, which],
+                relay_send.at[stage], relay_recv.at[stage, f, 0 if which == slice(None) else which],
+                (0, toward, 0),
+            ).start()
+        elif reader:
+            source = {0: 0, 1: 2, NX - 1: 1}[dx]
+            remote(
+                part_out.at[stage, reader, which], part_in.at[stage, source * 2 + f, which],
+                p_send.at[stage], p_recv.at[stage], (0, dx, f),
+            ).start()
+
     def partial(stage, reader):
-        feat = feats[stage]
-        last = stage == STAGES - 1
         dx, f = reader // 2, reader % 2
         relays = (dx, f) in ((1, 0), (NX - 1, 1))
-        if relays and not last:
+        if relays:
             land(relay_in.at[stage, f], relay_recv.at[stage, f, 0])
 
-        def send(which):
-            if dx == 2:
-                toward = 1 if f == 0 else NX - 1
-                remote(
-                    part_out.at[stage, reader, which], relay_in.at[stage, f, which],
-                    relay_send.at[stage], relay_recv.at[stage, f, which if last else 0],
-                    (0, toward, 0),
-                ).start()
-            elif reader:
-                source = {0: 0, 1: 2, NX - 1: 1}[dx]
-                remote(
-                    part_out.at[stage, reader, which], part_in.at[stage, source * 2 + f, which],
-                    p_send.at[stage], p_recv.at[stage], (0, dx, f),
-                ).start()
-
         def one(i, carry):
-            first = (reader * blocks + i) * slots
-            left = jnp.concatenate([tiles_all[reader, i, k] for k in range(slots)], axis=1)
-            right = jnp.concatenate([feat[table[first + k]] for k in range(slots)], axis=0)
-            total = dot(left, right)
+            total = product(stage, reader, i)
             if relays:
-                if last:
-                    land(relay_in.at[stage, f, i], relay_recv.at[stage, f, i])
                 total += relay_in[stage, f, i].astype(f32)
             part_out[stage, reader, i] = total.astype(bf16)
-            if last:
-                send(i)
             return carry
 
-        if last:
+        lax.fori_loop(0, blocks, one, 0)
+        send_part(stage, reader)
+
+    def last_partials():
+        stage = STAGES - 1
+        for reader in (4, 5, 3, 6):
+            totals = [product(stage, reader, i) for i in range(blocks)]
             for i in range(blocks):
-                one(i, 0)
-        else:
-            lax.fori_loop(0, blocks, one, 0)
-            send(slice(None))
+                part_out[stage, reader, i] = totals[i].astype(bf16)
+            if reader // 2 == 2:
+                for i in range(blocks):
+                    send_part(stage, reader, i)
+            else:
+                send_part(stage, reader)
+        relayed = (2, 7)
+        for reader in relayed:
+            for i in range(blocks):
+                relay_sum[reader % 2, i] = product(stage, reader, i)
+        for i in range(blocks):
+            for reader in relayed:
+                f = reader % 2
+                land(relay_in.at[stage, f, i], relay_recv.at[stage, f, i])
+                total = relay_sum[f, i] + relay_in[stage, f, i].astype(f32)
+                part_out[stage, reader, i] = total.astype(bf16)
+                send_part(stage, reader, i)
+        for reader in (1, 0):
+            for i in range(blocks):
+                part_out[stage, reader, i] = product(stage, reader, i).astype(bf16)
+            send_part(stage, reader)
 
     def column_chunk(stage, flip):
         return (other if flip else core) * 2 + stage % 2
@@ -306,13 +327,20 @@
         store_grad(1, dot(mixed_two, back_two, ((0,), (0,))))
         store_grad(0, dot(mixed_one_ref[...], back_one, ((0,), (0,))))
 
+    turns = {(stage, m): [] for stage in range(STAGES) for m in range(NZ - 1)}
+    for m, dx, f in ((0, 0, 1), (1, 0, 0), (2, 1, 1), (3, 3, 0), (5, 2, 0), (6, 2, 1)):
+        turns[1, m].append((0, dx, f))
+    turns[2, 2].append((0, 1, 0))
+    turns[2, 3].append((0, 3, 1))
     order = [(2, 0), (2, 1), (1, 1), (3, 0), (1, 0), (3, 1), (0, 1), (0, 0)]
-    first_order = [(0, 1), (0, 0), (1, 1), (3, 0), (2, 0), (2, 1), (1, 0), (3, 1)]
+    for stage in range(2, STAGES):
+        for turn, (dx, f) in enumerate(order):
+            turns[stage, min(turn, NZ - 2)].append((stage - 1, dx, f))
 
     for stage in range(STAGES):
         for m in range(NZ - 1):
             ring_tick(stage, m)
-            if m == 2 and stage + 1 < STAGES:
+            if m == 4 and stage + 1 < STAGES:
                 start_stage(stage + 1)
             if stage == 0:
                 if m == 1:
@@ -335,28 +363,22 @@
                     for i in range(blocks):
                         land(tile_slot(1, 1, i), t_sib.at[1, i])
                         land(tile_slot(NX - 1, 1, i), t_sib.at[NX - 1, i])
-                if m == 4:
+                if m == 5:
                     for i in range(blocks):
                         land(tile_slot(2, 0, i), t_far.at[i])
                         share_tiles(2, i)
-                if m == 5:
+                if m == 6:
                     for i in range(blocks):
                         land(tile_slot(2, 1, i), t_sib.at[2, i])
-            turns = [m] if m < NZ - 2 else [m, m + 1]
-            for turn in turns:
-                dx, f = (first_order if stage == 1 else order)[turn]
-                partial(stage - 1, dx * 2 + f)
-            if stage == STAGES - 1:
-                if m == 0:
-                    finish_one(0)
-                if m == 2:
-                    finish_one(1)
-                if m >= 3:
-                    layer_one(m - 3)
+            for of, dx, f in turns[stage, m]:
+                partial(of, dx * 2 + f)
         land(feat_slot(stage, 0, 1), sib_recv.at[stage])
         land(feat_slot(stage, 0, 0), own_sem.at[stage])
-    for dx, f in order:
-        partial(STAGES - 1, dx * 2 + f)
+    last_partials()
+    for stage in range(2):
+        finish_one(stage)
+    for i in range(blocks):
+        layer_one(i)
     start_two()
     finish_two(2)
     finish_two(3)
@@ -405,29 +427,27 @@
         for n in range(NX - 1):
             value += second_in[h, n].astype(f32)
         for n, (r, q) in enumerate(tiles_of):
-            third[h, n] = value[r * 8 : (r + 1) * 8, q * wide : (q + 1) * wide]
-        for dz in range(1, NZ):
-            remote(
-                third.at[h, lax.rem(my_z + dz, NZ)], third_in.at[h, NZ - dz - 1],
-                third_send, third_recv.at[h], (dz, 0, 0),
-            ).start()
+            third[n, h] = value[r * 8 : (r + 1) * 8, q * wide : (q + 1) * wide]
+    for dz in (4, 3, 5, 2, 6, 1, 7):
+        remote(
+            third.at[lax.rem(my_z + dz, NZ)], third_in.at[NZ - dz - 1],
+            third_send, third_recv, (dz, 0, 0),
+        ).start()
+    value = third[my_z]
+    land(third_in, third_recv)
+    for n in range(NZ - 1):
+        value += third_in[n]
+    third_done[my_z] = value
+    for dz in (4, 3, 5, 2, 6, 1, 7):
+        remote(
+            third_done.at[my_z], third_done.at[my_z], done_send, done_recv, (dz, 0, 0)
+        ).start()
+    land(third_done.at[pl.ds(0, NZ - 1)], done_recv)
+
     for h in range(2):
-        value = third[h, my_z]
-        land(third_in.at[h], third_recv.at[h])
-        for n in range(NZ - 1):
-            value += third_in[h, n]
-        third_done[h, my_z] = value
-        for dz in range(1, NZ):
-            remote(
-                third_done.at[h, my_z], third_done.at[h, my_z],
-                done_send, done_recv.at[h], (dz, 0, 0),
-            ).start()
-
-    for h in range(2):
-        land(third_done.at[h, pl.ds(0, NZ - 1)], done_recv.at[h])
         value = jnp.concatenate(
             [
-                jnp.concatenate([third_done[h, r * 4 + q] for q in range(4)], axis=1)
+                jnp.concatenate([third_done[r * 4 + q, h] for q in range(4)], axis=1)
                 for r in range(part // 8)
             ],
             axis=0,
@@ -509,6 +529,7 @@
             pltpu.VMEM((STAGES, 2 * NX, blocks, size, wide), bf16),
             pltpu.VMEM((STAGES, 6, blocks, size, wide), bf16),
             pltpu.VMEM((STAGES, 2, blocks, size, wide), bf16),
+            pltpu.VMEM((2, blocks, size, wide), f32),
             pltpu.VMEM((metas, 8, 128), jnp.int32),
             pltpu.SMEM((metas, 8, 128), jnp.int32),
             pltpu.SMEM((2 * NX * blocks * slots,), jnp.int32),
@@ -527,9 +548,9 @@
             pltpu.VMEM((2, quarter, width), f32),
             pltpu.VMEM((2, quarter, width), bf16),
             pltpu.VMEM((2, NX - 1, part, width), bf16),
-            pltpu.VMEM((2, NZ, 8, wide), f32),
-            pltpu.VMEM((2, NZ - 1, 8, wide), f32),
-            pltpu.VMEM((2, NZ, 8, wide), f32),
+            pltpu.VMEM((NZ, 2, 8, wide), f32),
+            pltpu.VMEM((NZ - 1, 2, 8, wide), f32),
+            pltpu.VMEM((NZ, 2, 8, wide), f32),
             dma((STAGES, 2, NZ - 1)),
             dma((STAGES,)),
             dma((STAGES,)),
@@ -552,9 +573,9 @@
             dma,
             dma((2,)),
             dma,
-            dma((2,)),
-            dma,
-            dma((2,)),
+            dma,
+            dma,
+            dma,
             dma,
             dma((2,)),
             dma,

time: 160 us -> 155 us (0.969)
  Pallas kernels: 156 us -> 150 us
    pallas_call x1, Pallas kernels: 156 us -> 150 us  [layers(): pl.pallas_call(layers_kernel, out_shape=(jax.ShapeDtypeStruct((rows, widt...]
where the time goes in v3:
time: 155 us
  Pallas kernels  150 us (97%)
  other arithmetic  2.87 us (2%)
    pallas_call x1, Pallas kernels, layers(): pl.pallas_call(layers_kernel, out_shape=(jax.ShapeDtypeStruct((rows, widt...  150 us

profile of v3, /device:TPU:1, one launch (start us, length us, event | category | flops | bytes accessed | tf_op | source)
XLA Modules:
  0.0 154.5 jit_solution(8028984912044690526)
XLA Ops:
  0.6 150.2 %layers.1 = (bf16[512,512]{1,0:T(8,128)(2,1)}, bf16[2,512,512]{2,1,0:T(8,128)(2,1)}) custom-call(bf16[4,128,512]{2,1,0:T(8,128)(2,1)} %bitcast.13, bf16[4,128,512]{2,1,0:T(8,128)(2,1)} %bitcast.14, bf16[4,8,128,128]{3,2,1,0:T(8,128)(2,1)} %bitcast.12, s32[4,8]{1,0:T(4,128)} %bitcast.16, s32[1,64]{1,0:T(1,128)} %bitcast.17, bf16[512,512]{1,0:T(8,128)(2,1)} %one_ref.1, ...), custom_call_target="tpu_custom_call" | custom-call | flops 7000000000 | bytes 8388608 | tf_op jit(solution)/shard_map/layers/pallas_call | solution.py:518
  150.9 0.0 copy-start
  150.9 2.9 %multiply_bitcast_fusion = (f32[512,512]{1,0:T(8,128)}, f32[512,512]{1,0:T(8,128)}) fusion(bf16[2,512,512]{2,1,0:T(8,128)(2,1)} %get-tuple-element.6), kind=kLoop, calls=%fused_computation | loop fusion | flops 1048576 | bytes 3145728 | tf_op jit(solution)/shard_map/mul | solution.py:605
  153.7 0.0 copy-done
  153.7 0.8 copy.12
Async XLA Ops:
  150.9 2.9 %copy-start = (bf16[512,512]{1,0:T(8,128)(2,1)S(1)}, bf16[512,512]{1,0:T(8,128)(2,1)}, u32[]{:S(2)}) copy-start(bf16[512,512]{1,0:T(8,128)(2,1)} %get-tuple-element.5) | copy-start | bytes 1572868

commit v4 on v3

--- a/solution.py
+++ b/solution.py
@@ -173,18 +173,20 @@
             reader_index = dom_index(my_z, lax.rem(my_x + dx, NX), other if f else core)
 
             def entry(n, carry):
-                col = metas_smem[reader, n // slots, n % slots]
+                col = metas_smem[reader, lax.div(n, slots), lax.rem(n, slots)]
                 owner = jnp.maximum(col - blocks, 0)
-                valid = (col >= blocks) & ((owner // 2) % NX == my_x)
-                dz = (owner // (2 * NX) - my_z + NZ) % NZ
-                flip = (owner + core) % 2
-                where = jnp.where(dz == 0, flip, 2 * NX + (dz - 1) * 2 + flip)
+                chip = lax.div(owner, 2)
+                valid = (col >= blocks) & (lax.rem(chip, NX) == my_x)
+                dz = lax.rem(lax.div(chip, NX) + (NZ - my_z), NZ)
+                flip = lax.rem(owner + core, 2)
+                place = dz * 2 + flip
+                where = jnp.where(dz == 0, flip, place + (2 * NX - 2))
                 block = metas_smem[where, blocks, reader_index]
-                slot = (dz * 2 + flip) * blocks + block
+                slot = place * blocks + block
                 table[reader * blocks * slots + n] = jnp.where(valid, slot, 2 * NZ * blocks)
                 return carry
 
-            lax.fori_loop(0, blocks * slots, entry, 0)
+            lax.fori_loop(0, blocks * slots, entry, 0, unroll=slots)
 
     def build_local(i):
         sums = [jnp.zeros((size, size), f32) for _ in range(blocks)]
@@ -340,15 +342,14 @@
     for stage in range(STAGES):
         for m in range(NZ - 1):
             ring_tick(stage, m)
-            if m == 4 and stage + 1 < STAGES:
+            if m == 5 and stage + 1 < STAGES:
                 start_stage(stage + 1)
             if stage == 0:
                 if m == 1:
                     send_tiles(range(blocks // 2, blocks))
                     copy_metas()
-                if m >= 2 and m < 6:
-                    build_table((2 * (m - 2), 2 * (m - 2) + 1))
-                    build_local(m - 2)
+                if m in (2, 3, 4, 6):
+                    build_table({2: (1, 0), 3: (3, 6), 4: (4, 5), 6: (2, 7)}[m])
                 if m == 5:
                     pass_tiles(range(blocks // 2))
                 continue
@@ -378,6 +379,7 @@
     for stage in range(2):
         finish_one(stage)
     for i in range(blocks):
+        build_local(i)
         layer_one(i)
     start_two()
     finish_two(2)
@@ -593,6 +595,30 @@
     )(initial, history, tiles, cols, chosen, weight_one, weight_two, cotangent)
 
 
+def finish_kernel(sum_ref, rows_ref, one_ref, two_ref, out_ref):
+    one_ref[...] = BETA_ONE * sum_ref[0].astype(jnp.float32)
+    two_ref[...] = BETA_TWO * sum_ref[1].astype(jnp.float32)
+    out_ref[...] = rows_ref[...]
+
+
+def finish(summed, output):
+    width = summed.shape[1]
+    rows = output.shape[0]
+    steps = 4
+    grad = pl.BlockSpec((width // steps, width), lambda n: (n, 0))
+    out = pl.BlockSpec((rows // steps, width), lambda n: (n, 0))
+    full = jax.ShapeDtypeStruct((width, width), jnp.float32)
+    return pl.pallas_call(
+        finish_kernel,
+        grid=(steps,),
+        out_shape=(full, full, jax.ShapeDtypeStruct(output.shape, output.dtype)),
+        in_specs=[pl.BlockSpec((2, width // steps, width), lambda n: (0, n, 0)), out],
+        out_specs=(grad, grad, out),
+        compiler_params=pltpu.CompilerParams(vmem_limit_bytes=56 * 2**20),
+        name="finish",
+    )(summed, output)
+
+
 def local(initial, history, tile_values, tile_cols, send_blocks, weight_one, weight_two, cotangent):
     tiles = tile_values[0]
     blocks, slots, size, _ = tiles.shape
@@ -601,8 +627,7 @@
         initial[0].reshape(blocks, size, width), history[0].reshape(blocks, size, width),
         tiles, tile_cols[0], send_blocks[0], weight_one, weight_two, cotangent[0],
     )
-    grad_one = BETA_ONE * summed[0].astype(jnp.float32)
-    grad_two = BETA_TWO * summed[1].astype(jnp.float32)
+    grad_one, grad_two, output = finish(summed, output)
     return (output[None], grad_one, grad_two)
 
 

time: 155 us -> 155 us (level)
  Pallas kernels: 150 us -> 154 us
  other arithmetic: 2.87 us -> 0 us
    pallas_call x0 -> x1, Pallas kernels: none -> 3.77 us  [finish(): pl.pallas_call(finish_kernel, grid=(steps,), out_shape=(full, full, jax.S...]
    mul x1 -> x0, other arithmetic: 2.87 us -> none  [local(): grad_two = BETA_TWO * summed[1].astype(jnp.float32)]
where the time goes in v4:
time: 155 us
  Pallas kernels  154 us (99%)
    pallas_call x1, Pallas kernels, layers(): pl.pallas_call(layers_kernel, out_shape=(jax.ShapeDtypeStruct((rows, widt...  150 us
    pallas_call x1, Pallas kernels, finish(): pl.pallas_call(finish_kernel, grid=(steps,), out_shape=(full, full, jax.S...  3.77 us

profile of v4, /device:TPU:1, one launch (start us, length us, event | category | flops | bytes accessed | tf_op | source)
XLA Modules:
  0.0 154.8 jit_solution(4860184252985486957)
XLA Ops:
  0.6 150.4 %layers.1 = (bf16[512,512]{1,0:T(8,128)(2,1)}, bf16[2,512,512]{2,1,0:T(8,128)(2,1)}) custom-call(bf16[4,128,512]{2,1,0:T(8,128)(2,1)} %bitcast.8, bf16[4,128,512]{2,1,0:T(8,128)(2,1)} %bitcast.9, bf16[4,8,128,128]{3,2,1,0:T(8,128)(2,1)} %bitcast.7, s32[4,8]{1,0:T(4,128)} %bitcast.12, s32[1,64]{1,0:T(1,128)} %bitcast.13, bf16[512,512]{1,0:T(8,128)(2,1)} %one_ref.1, ...), custom_call_target="tpu_custom_call" | custom-call | flops 7000000000 | bytes 8388608 | tf_op jit(solution)/shard_map/layers/pallas_call | solution.py:520
  151.0 3.8 %finish.1 = (f32[512,512]{1,0:T(8,128)}, f32[512,512]{1,0:T(8,128)}, bf16[512,512]{1,0:T(8,128)(2,1)}) custom-call(bf16[2,512,512]{2,1,0:T(8,128)(2,1)} %get-tuple-element.8.sum_ref, bf16[512,512]{1,0:T(8,128)(2,1)} %get-tuple-element.9.rows_ref), custom_call_target="tpu_custom_call" | custom-call | tf_op jit(solution)/shard_map/finish/pallas_call | solution.py:611

commit v5 on v4

--- a/solution.py
+++ b/solution.py
@@ -31,14 +31,14 @@
 
 
 def layers_kernel(
-    initial_ref, history_ref, tiles_ref, cols_ref, chosen_ref, one_ref, two_ref, cot_ref,
-    out_ref, sum_ref,
+    initial_ref, history_ref, tiles_ref, cols_ref, chosen_ref, one_any, two_any, cot_any,
+    out_ref, sum_ref, one_ref, two_ref, cot_ref, load_sem,
     feat0, feat1, feat2, feat3, tiles_all, part_out, part_in, relay_in, relay_sum, metas, metas_smem, table,
     local_ref, base_ref, received_ref, mixed_one_ref, mixed_two_ref, hidden_ref, slope_ref,
     grad_ref, send_ref, pair_in, pair_sum, first_in, first_sum, first_out, second_in,
     third, third_in, third_done,
     z_recv, sib_recv, z_send, own_sem, t_recv, t_far, t_sib, t_send, t_own, p_recv, p_send,
-    relay_recv, relay_send, m_recv, m_send, m_copy, pair_sems, first_send, first_recv,
+    relay_recv, relay_send, m_recv, m_send, m_copy, pair_send, pair_recv, first_send, first_recv,
     second_send, second_recv, third_send, third_recv, done_send, done_recv,
     gather_send, gather_recv, share_send, share_recv, back_send, back_recv,
 ):
@@ -155,6 +155,12 @@
         remote(metas.at[0], metas.at[slot], m_send, m_recv, peer).start()
     for i in range(blocks):
         remote(tiles_ref.at[i], tile_slot(0, 1, i), t_send, t_sib.at[0, i], (0, 0, 1)).start()
+    loads = [
+        pltpu.make_async_copy(src, dst, load_sem.at[n])
+        for n, (src, dst) in enumerate(((one_any, one_ref), (two_any, two_ref), (cot_any, cot_ref)))
+    ]
+    for load in loads:
+        load.start()
     send_tiles(range(blocks // 2))
     own_tiles = pltpu.make_async_copy(tiles_ref, tiles_all.at[0], t_own)
     own_tiles.start()
@@ -233,7 +239,7 @@
             part_out[stage, reader, i] = total.astype(bf16)
             return carry
 
-        lax.fori_loop(0, blocks, one, 0)
+        lax.fori_loop(0, blocks, one, 0, unroll=blocks)
         send_part(stage, reader)
 
     def last_partials():
@@ -355,6 +361,8 @@
                 continue
             if stage == 1:
                 if m == 0:
+                    for load in loads:
+                        load.wait()
                     own_tiles.wait()
                     for i in range(blocks):
                         land(tile_slot(0, 1, i), t_sib.at[0, i])
@@ -386,10 +394,6 @@
     finish_two(3)
     layer_two()
 
-    remote(send_ref.at[other], pair_in, pair_sems.at[0], pair_sems.at[1], (0, 0, 1)).start()
-    land(pair_in, pair_sems.at[1])
-    pair_sum[...] = (grad_ref[core] + pair_in[...].astype(f32)).astype(bf16)
-
     half = width // 2
     quarter = half // NX
     part = quarter // NX
@@ -401,8 +405,16 @@
     def along(h, turn, d):
         return (0, d, 0) if h == turn else (0, 0, 0, d)
 
-    for d in (2, 1, 3):
-        for h in range(2):
+    for h in range(2):
+        here = pl.ds(h * half, half)
+        remote(
+            send_ref.at[other, here], pair_in.at[here], pair_send, pair_recv.at[h], (0, 0, 1)
+        ).start()
+    for h in range(2):
+        here = pl.ds(h * half, half)
+        land(pair_in.at[here], pair_recv.at[h])
+        pair_sum[here, :] = (grad_ref[core, here, :] + pair_in[here, :].astype(f32)).astype(bf16)
+        for d in (2, 1, 3):
             theirs = rows_at(h * half + lax.rem(place[h][0] + d, NX) * quarter, quarter)
             remote(
                 pair_sum.at[theirs], first_in.at[h, NX - d - 1],
@@ -495,7 +507,7 @@
         land(relay_in.at[stage], relay_send.at[stage])
     land(metas.at[pl.ds(1, len(near))], m_send)
     land(tiles_all.at[pl.ds(1, 2 * NX - 1)], t_send)
-    land(pair_in, pair_sems.at[0])
+    land(pair_in, pair_send)
     land(first_in, first_send)
     land(second_in, second_send)
     land(third_in, third_send)
@@ -523,9 +535,11 @@
             jax.ShapeDtypeStruct((rows, width), bf16),
             jax.ShapeDtypeStruct((2, width, width), bf16),
         ),
-        in_specs=[vmem] * 8,
+        in_specs=[vmem] * 5 + [pl.BlockSpec(memory_space=pl.ANY)] * 3,
         out_specs=(vmem, vmem),
-        scratch_shapes=[pltpu.VMEM((2 * NZ * blocks + 1, size, wide), bf16)] * STAGES
+        scratch_shapes=[pltpu.VMEM((width, width), bf16)] * 2
+        + [pltpu.VMEM((rows, width), bf16), dma((3,))]
+        + [pltpu.VMEM((2 * NZ * blocks + 1, size, wide), bf16)] * STAGES
         + [
             pltpu.VMEM((2 * NX, blocks, slots, size, size), bf16),
             pltpu.VMEM((STAGES, 2 * NX, blocks, size, wide), bf16),
@@ -569,6 +583,7 @@
             dma,
             dma,
             dma,
+            dma,
             dma((2,)),
             dma,
             dma((2,)),
@@ -604,7 +619,7 @@
 def finish(summed, output):
     width = summed.shape[1]
     rows = output.shape[0]
-    steps = 4
+    steps = 2
     grad = pl.BlockSpec((width // steps, width), lambda n: (n, 0))
     out = pl.BlockSpec((rows // steps, width), lambda n: (n, 0))
     full = jax.ShapeDtypeStruct((width, width), jnp.float32)

time: 155 us -> 152 us (0.981)
  Pallas kernels: 154 us -> 151 us
    pallas_call x1, Pallas kernels: 150 us -> 148 us  [layers(): pl.pallas_call(layers_kernel, out_shape=(jax.ShapeDtypeStruct((rows, widt...]
where the time goes in v5:
time: 152 us
  Pallas kernels  151 us (99%)
    pallas_call x1, Pallas kernels, layers(): pl.pallas_call(layers_kernel, out_shape=(jax.ShapeDtypeStruct((rows, widt...  148 us

profile of v5, /device:TPU:1, one launch (start us, length us, event | category | flops | bytes accessed | tf_op | source)
XLA Modules:
  0.0 151.6 jit_solution(9194125326166779109)
XLA Ops:
  0.6 148.2 %layers.1 = (bf16[512,512]{1,0:T(8,128)(2,1)}, bf16[2,512,512]{2,1,0:T(8,128)(2,1)}) custom-call(bf16[4,128,512]{2,1,0:T(8,128)(2,1)} %bitcast.8, bf16[4,128,512]{2,1,0:T(8,128)(2,1)} %bitcast.9, bf16[4,8,128,128]{3,2,1,0:T(8,128)(2,1)} %bitcast.7, s32[4,8]{1,0:T(4,128)} %bitcast.12, s32[1,64]{1,0:T(1,128)} %bitcast.13, bf16[512,512]{1,0:T(8,128)(2,1)} %one_any.1, ...), custom_call_target="tpu_custom_call" | custom-call | flops 7000000000 | bytes 8388608 | tf_op jit(solution)/shard_map/layers/pallas_call | solution.py:532
  148.9 2.7 %finish.1 = (f32[512,512]{1,0:T(8,128)}, f32[512,512]{1,0:T(8,128)}, bf16[512,512]{1,0:T(8,128)(2,1)}) custom-call(bf16[2,512,512]{2,1,0:T(8,128)(2,1)} %get-tuple-element.8.sum_ref, bf16[512,512]{1,0:T(8,128)(2,1)} %get-tuple-element.9.rows_ref), custom_call_target="tpu_custom_call" | custom-call | tf_op jit(solution)/shard_map/finish/pallas_call | solution.py:626

commit v6 on v5

--- a/solution.py
+++ b/solution.py
@@ -476,7 +476,7 @@
     for h in range(2):
         land(second_in.at[h], gather_recv.at[h])
         mine = rows_at(h * half + place[h][0] * quarter, quarter)
-        for d in (2, 1, 3):
+        for d in (1, 3):
             remote(
                 sum_ref.at[core, mine], sum_ref.at[core, mine],
                 share_send, share_recv.at[h, NX - d - 1], along(h, 0, d),
@@ -493,6 +493,13 @@
         for h in range(2):
             got = share_at(h, d)
             land(sum_ref.at[core, got], share_recv.at[h, d - 1])
+            if d != 2:
+                start = h * half + lax.rem(place[h][0] + d, NX) * quarter
+                piece = rows_at(start + (quarter // 2 if d == 1 else 0), quarter // 2)
+                remote(
+                    sum_ref.at[core, piece], sum_ref.at[core, piece],
+                    share_send, share_recv.at[h, 1], along(h, 0, NX - d),
+                ).start()
             remote(
                 sum_ref.at[core, got], sum_ref.at[core, got],
                 back_send, back_recv.at[h, d], (0, 0, 1),

time: 152 us -> 154 us (1.013)
  Pallas kernels: 151 us -> 153 us
    pallas_call x1, Pallas kernels: 148 us -> 151 us  [layers(): pl.pallas_call(layers_kernel, out_shape=(jax.ShapeDtypeStruct((rows, widt...]
where the time goes in v6:
time: 154 us
  Pallas kernels  153 us (99%)
    pallas_call x1, Pallas kernels, layers(): pl.pallas_call(layers_kernel, out_shape=(jax.ShapeDtypeStruct((rows, widt...  151 us

profile of v6, /device:TPU:1, one launch (start us, length us, event | category | flops | bytes accessed | tf_op | source)
XLA Modules:
  0.0 154.0 jit_solution(13271056592133683149)
XLA Ops:
  0.6 150.7 %layers.1 = (bf16[512,512]{1,0:T(8,128)(2,1)}, bf16[2,512,512]{2,1,0:T(8,128)(2,1)}) custom-call(bf16[4,128,512]{2,1,0:T(8,128)(2,1)} %bitcast.8, bf16[4,128,512]{2,1,0:T(8,128)(2,1)} %bitcast.9, bf16[4,8,128,128]{3,2,1,0:T(8,128)(2,1)} %bitcast.7, s32[4,8]{1,0:T(4,128)} %bitcast.12, s32[1,64]{1,0:T(1,128)} %bitcast.13, bf16[512,512]{1,0:T(8,128)(2,1)} %one_any.1, ...), custom_call_target="tpu_custom_call" | custom-call | flops 7000000000 | bytes 8388608 | tf_op jit(solution)/shard_map/layers/pallas_call | solution.py:539
  151.3 2.7 %finish.1 = (f32[512,512]{1,0:T(8,128)}, f32[512,512]{1,0:T(8,128)}, bf16[512,512]{1,0:T(8,128)(2,1)}) custom-call(bf16[2,512,512]{2,1,0:T(8,128)(2,1)} %get-tuple-element.8.sum_ref, bf16[512,512]{1,0:T(8,128)(2,1)} %get-tuple-element.9.rows_ref), custom_call_target="tpu_custom_call" | custom-call | tf_op jit(solution)/shard_map/finish/pallas_call | solution.py:633

commit v7 on v5

--- a/solution.py
+++ b/solution.py
@@ -31,8 +31,8 @@
 
 
 def layers_kernel(
-    initial_ref, history_ref, tiles_ref, cols_ref, chosen_ref, one_any, two_any, cot_any,
-    out_ref, sum_ref, one_ref, two_ref, cot_ref, load_sem,
+    initial_ref, history_any, tiles_ref, cols_ref, chosen_ref, one_any, two_any, cot_any,
+    out_ref, sum_ref, history_ref, one_ref, two_ref, cot_ref, load_sem,
     feat0, feat1, feat2, feat3, tiles_all, part_out, part_in, relay_in, relay_sum, metas, metas_smem, table,
     local_ref, base_ref, received_ref, mixed_one_ref, mixed_two_ref, hidden_ref, slope_ref,
     grad_ref, send_ref, pair_in, pair_sum, first_in, first_sum, first_out, second_in,
@@ -157,7 +157,7 @@
         remote(tiles_ref.at[i], tile_slot(0, 1, i), t_send, t_sib.at[0, i], (0, 0, 1)).start()
     loads = [
         pltpu.make_async_copy(src, dst, load_sem.at[n])
-        for n, (src, dst) in enumerate(((one_any, one_ref), (two_any, two_ref), (cot_any, cot_ref)))
+        for n, (src, dst) in enumerate(((one_any, one_ref), (two_any, two_ref), (cot_any, cot_ref), (history_any, history_ref)))
     ]
     for load in loads:
         load.start()
@@ -197,7 +197,7 @@
     def build_local(i):
         sums = [jnp.zeros((size, size), f32) for _ in range(blocks)]
         for k in range(slots):
-            tile = tiles_ref[i, k].astype(f32)
+            tile = tiles_all[0, i, k].astype(f32)
             for c in range(blocks):
                 mask = jnp.where(metas_smem[0, i, k] == c, 1.0, 0.0).astype(f32)
                 sums[c] += tile * mask
@@ -525,6 +525,7 @@
     quarter = width // 2 // NX
     part = quarter // NX
     vmem = pl.BlockSpec(memory_space=pltpu.VMEM)
+    far = pl.BlockSpec(memory_space=pl.ANY)
     dma = pltpu.SemaphoreType.DMA
     bf16 = jnp.bfloat16
     f32 = jnp.float32
@@ -535,10 +536,11 @@
             jax.ShapeDtypeStruct((rows, width), bf16),
             jax.ShapeDtypeStruct((2, width, width), bf16),
         ),
-        in_specs=[vmem] * 5 + [pl.BlockSpec(memory_space=pl.ANY)] * 3,
+        in_specs=[vmem, far, far, vmem, vmem, far, far, far],
         out_specs=(vmem, vmem),
-        scratch_shapes=[pltpu.VMEM((width, width), bf16)] * 2
-        + [pltpu.VMEM((rows, width), bf16), dma((3,))]
+        scratch_shapes=[pltpu.VMEM((blocks, size, width), bf16)]
+        + [pltpu.VMEM((width, width), bf16)] * 2
+        + [pltpu.VMEM((rows, width), bf16), dma((4,))]
         + [pltpu.VMEM((2 * NZ * blocks + 1, size, wide), bf16)] * STAGES
         + [
             pltpu.VMEM((2 * NX, blocks, slots, size, size), bf16),

time: 152 us -> 151 us (level)
  no operation moved by 1% of the time
where the time goes in v7:
time: 151 us
  Pallas kernels  150 us (99%)
    pallas_call x1, Pallas kernels, layers(): pl.pallas_call(layers_kernel, out_shape=(jax.ShapeDtypeStruct((rows, widt...  148 us

profile of v7, /device:TPU:1, one launch (start us, length us, event | category | flops | bytes accessed | tf_op | source)
XLA Modules:
  0.0 151.1 jit_solution(6357942766971336473)
XLA Ops:
  0.6 147.7 %layers.1 = (bf16[512,512]{1,0:T(8,128)(2,1)}, bf16[2,512,512]{2,1,0:T(8,128)(2,1)}) custom-call(bf16[4,128,512]{2,1,0:T(8,128)(2,1)} %bitcast.8, bf16[4,128,512]{2,1,0:T(8,128)(2,1)} %bitcast.9, bf16[4,8,128,128]{3,2,1,0:T(8,128)(2,1)} %bitcast.7, s32[4,8]{1,0:T(4,128)} %bitcast.12, s32[1,64]{1,0:T(1,128)} %bitcast.13, bf16[512,512]{1,0:T(8,128)(2,1)} %one_any.1, ...), custom_call_target="tpu_custom_call" | custom-call | flops 7000000000 | bytes 8388608 | tf_op jit(solution)/shard_map/layers/pallas_call | solution.py:533
  148.4 2.7 %finish.1 = (f32[512,512]{1,0:T(8,128)}, f32[512,512]{1,0:T(8,128)}, bf16[512,512]{1,0:T(8,128)(2,1)}) custom-call(bf16[2,512,512]{2,1,0:T(8,128)(2,1)} %get-tuple-element.8.sum_ref, bf16[512,512]{1,0:T(8,128)(2,1)} %get-tuple-element.9.rows_ref), custom_call_target="tpu_custom_call" | custom-call | tf_op jit(solution)/shard_map/finish/pallas_call | solution.py:628
